TPU v7x, 32 devices: a whole 2x2x4 slice. The times are simulated.
32 devices in a mesh: ctx: 8 (over y, x, core), feat: 4 (over z).
Axes of the slice: x: 2, y: 2, z: 4, core: 2. Of those that a mesh axis runs over, the one named last changes fastest.
Arguments:
- tokens: bfloat16 [4, 2048, 8192], P(None, 'ctx', 'feat'), may hold values from -128 to 128
- norm_gain: float32 [8192], P('feat'), may hold values from 0.1 to 1.9
- qkv_weight: bfloat16 [3, 32, 6, 256, 256], P(None, 'feat'), may hold values from -1 to 1
- out_weight: bfloat16 [32, 6, 256, 256], P('feat'), may hold values from -0.15625 to 0.15625
- section_bits: int32 [5], replicated, may hold values from 0 to 4, each once
- positions: int32 [4, 2048], P(None, 'ctx'), may hold values from 0 to 128, as said below
Outputs:
- layer_out: float32 [4, 2048, 8192], P(None, 'ctx', 'feat')
Inputs may be any that keep to these rules, and one draw needn't show every extreme that they name: Within a document, positions rise by one from token to token until they reach 128, where they stay; a document starts at position 0, except the first of a sequence, which may start above 0.
All inputs are finite; a program needn't handle non-finite values.
Results may differ from a plain program's by a relative error of at most 0.0064.
Values may be sent and summed in bfloat16 or wider, within the bound.
A program may use at most 256 MiB of HBM per device.

v0:
```python
import jax
import jax.numpy as jnp
from jax import lax
from jax.sharding import PartitionSpec as P

D = 8192
WINDOW = 128
HEAD = 128


def swapped(value, axis, bit):
    mask = 2**bit
    pairs = [(source, source ^ mask) for source in range(lax.axis_size(axis))]
    return lax.ppermute(value, axis, pairs)


def passed_along(shard, axis, by):
    devices = lax.axis_size(axis)
    pairs = [(i, i + by) for i in range(devices) if 0 <= i + by < devices]
    return lax.ppermute(shard, axis, pairs)


def butterfly(blocks, weight, section_bits):
    rows, local_blocks, block = blocks.shape
    local_bits = local_blocks.bit_length() - 1
    device_bits = lax.axis_size("feat").bit_length() - 1
    section_count = section_bits.shape[0]
    section_ids = jnp.arange(section_count, dtype=jnp.int32)
    total = jnp.einsum(
        "rlk,mlkj->mrlj", blocks, weight[:, :, 0], preferred_element_type=jnp.float32
    )
    for bit in range(local_bits + device_bits):
        if bit < local_bits:
            split = blocks.reshape(rows, local_blocks // (2 << bit), 2, 1 << bit, block)
            partner = split[:, :, ::-1].reshape(rows, local_blocks, block)
        else:
            partner = swapped(blocks, "feat", bit - local_bits)
        section = 1 + jnp.sum(jnp.where(section_bits == bit, section_ids, 0))
        chosen = lax.dynamic_index_in_dim(weight, section, axis=2, keepdims=False)
        total = total + jnp.einsum(
            "rlk,mlkj->mrlj", partner, chosen, preferred_element_type=jnp.float32
        )
    return total


def per_device(tokens, norm_gain, qkv_weight, out_weight, section_bits, positions):
    seqs, tok_rows, local_width = tokens.shape
    block = qkv_weight.shape[-1]
    local_blocks = local_width // block
    local_heads = local_width // HEAD
    x_full = tokens.astype(jnp.float32)
    row_squares = lax.psum(jnp.sum(x_full * x_full, axis=-1), "feat")
    mean_sq = row_squares / D
    normed = (x_full * lax.rsqrt(mean_sq[..., None] + 1e-05) * norm_gain).astype(jnp.bfloat16)
    blocks = normed.reshape(seqs * tok_rows, local_blocks, block)
    projected = butterfly(blocks, qkv_weight, section_bits).astype(jnp.bfloat16)
    projected = projected.reshape(3, seqs, tok_rows, local_heads, HEAD)
    query = projected[0]
    key_value = projected[1:3]
    tail = key_value[:, :, tok_rows - WINDOW :]
    rim = passed_along(tail, "ctx", 1)
    joined = jnp.concatenate([rim, key_value], axis=2)
    count = tok_rows // WINDOW
    kv_blocks = joined.reshape(2, seqs, count + 1, WINDOW, local_heads, HEAD)
    paired = jnp.concatenate([kv_blocks[:, :, :-1], kv_blocks[:, :, 1:]], axis=3)
    query_blocks = query.reshape(seqs, count, WINDOW, local_heads, HEAD)
    scores = jnp.einsum(
        "scqhd,sckhd->schqk", query_blocks, paired[0], preferred_element_type=jnp.float32
    )
    scores = scores * HEAD ** (-0.5)
    qpos = jnp.arange(WINDOW, dtype=jnp.int32)
    kpos = jnp.arange(2 * WINDOW, dtype=jnp.int32)
    block_ids = jnp.arange(count, dtype=jnp.int32)
    dist = qpos[:, None] + WINDOW - kpos[None, :]
    key_index = (
        lax.axis_index("ctx") * tok_rows + block_ids[:, None] * WINDOW + kpos[None, :] - WINDOW
    )
    valid = ((dist >= 0) & (dist < WINDOW))[None, None] & (key_index >= 0)[None, :, None, :]
    local_pos = positions.reshape(seqs, count, WINDOW)
    valid = valid & (dist[None, None] <= local_pos[..., None])
    masked = jnp.where(valid[:, :, None], scores, -1e30)
    top = jnp.max(masked, axis=-1, keepdims=True)
    expo = jnp.exp(masked - top)
    weights = (expo / jnp.sum(expo, axis=-1, keepdims=True)).astype(jnp.bfloat16)
    mixed = jnp.einsum("schqk,sckhd->scqhd", weights, paired[1], preferred_element_type=jnp.float32)
    attended = mixed.astype(jnp.bfloat16).reshape(seqs * tok_rows, local_blocks, block)
    result = butterfly(attended, out_weight[None], section_bits)[0]
    return x_full + result.reshape(seqs, tok_rows, local_width)


def solution(mesh):
    in_specs = (
        P(None, "ctx", "feat"),
        P("feat"),
        P(None, "feat", None, None, None),
        P("feat", None, None, None),
        P(),
        P(None, "ctx"),
    )
    out_specs = P(None, "ctx", "feat")
    return jax.shard_map(
        per_device, mesh=mesh, in_specs=in_specs, out_specs=out_specs, check_vma=False
    )
```

profile of v0, /device:TPU:2, one launch (start us, length us, event | category | flops | bytes accessed | tf_op | source)
XLA Modules:
  0.0 685.6 jit_solution(1325649548198439963)
XLA Ops:
  0.0 3.1 fusion.3
  3.1 12.0 %psum.7 = f32[4,256]{1,0:T(4,128)S(1)} all-reduce(f32[4,256]{1,0:T(4,128)S(1)} %fusion.3), channel_id=1, replica_groups=mesh['ctx'=8,'feat'=4] {'feat'}, use_global_device_ids=true, to_apply=%region_1.0 | all-reduce | flops 1024 | bytes 8192 | tf_op jit(solution)/shard_map/psum | solution.py:52
  15.1 3.2 fusion.5
  19.9 3.3 copy.45
  30.4 8.1 %reshape_reshape.20 = bf16[1024,1,2,4,256]{4,3,2,0,1:T(4,128)(2,1)} reshape(bf16[4,256,2048]{2,1,0:T(8,128)(2,1)} %copy-done) | data formatting | bytes 8388608 | tf_op jit(solution)/shard_map/reshape;reshape | solution.py:34
  38.5 7.8 %reshape_reshape.19 = bf16[1024,2,2,2,256]{4,3,2,1,0:T(2,128)(2,1)} reshape(bf16[4,256,2048]{2,1,0:T(8,128)(2,1)} %copy-done) | data formatting | bytes 8388608 | tf_op jit(solution)/shard_map/reshape;reshape | solution.py:34
  46.3 7.8 %reshape_reshape.18 = bf16[1024,4,2,1,256]{4,2,1,0,3:T(2,128)(2,1)} reshape(bf16[4,256,2048]{2,1,0:T(8,128)(2,1)} %copy-done) | data formatting | bytes 8388608 | tf_op jit(solution)/shard_map/reshape;reshape | solution.py:34
  54.1 12.2 %constant_dynamic-slice_fusion = (bf16[3,8,1,256,256]{4,3,2,1,0:T(8,128)(2,1)S(1)}, bf16[3,8,1,256,256]{4,3,2,1,0:T(8,128)(2,1)}, bf16[3,8,1,256,256]{4,3,2,1,0:...) fusion(bf16[3,8,6,256,256]{4,3,2,1,0:T(8,128)(2,1)} %param.8, ...), kind=kLoop, calls=%fused_computation.77 | loop fusion | bytes 37748756 | tf_op jit(solution)/shard_map/jit(dynamic_index_in_dim)/dynamic_slice | solution.py:39
  66.2 4.6 copy.44
  70.9 4.6 copy.41
  75.5 5.6 rev.20
  81.1 5.0 copy.42
  86.1 4.7 copy.38
  90.8 7.0 %rev.19 = bf16[1024,2,2,2,256]{4,3,2,1,0:T(2,128)(2,1)} reverse(bf16[1024,2,2,2,256]{4,3,2,1,0:T(2,128)(2,1)} %reshape_reshape.19), dimensions={2} | reverse | bytes 8388608 | tf_op jit(solution)/shard_map/rev | solution.py:35
  97.8 4.9 copy.39
  102.8 4.6 copy.35
  107.4 37.7 %rev.18 = bf16[1024,4,2,1,256]{4,2,1,0,3:T(2,128)(2,1)} reverse(bf16[1024,4,2,1,256]{4,2,1,0,3:T(2,128)(2,1)} %reshape_reshape.18), dimensions={2} | reverse | bytes 8388608 | tf_op jit(solution)/shard_map/rev | solution.py:35
  145.1 4.9 copy.36
  150.1 3.2 copy.47
  153.3 15.1 %fusion.24 = f32[8,3,256,1024]{2,3,1,0:T(8,128)} fusion(bf16[1024,8,256,1]{2,0,3,1:T(8,128)(2,1)} %bitcast.161, bf16[3,8,1,256,256]{3,4,0,1,2:T(8,128)(2,1)} %copy.41), kind=kOutput, calls=%fused_computation.44 | convolution fusion | flops 3221225472 | bytes 32505856 | tf_op jit(solution)/shard_map/rlk,mlkj->mrlj/dot_general | solution.py:40
  168.3 12.1 %fusion.26 = f32[8,3,256,1024]{2,3,1,0:T(8,128)} fusion(bf16[1024,8,256,1]{2,0,3,1:T(8,128)(2,1)S(1)} %bitcast.163, bf16[3,8,1,256,256]{3,4,0,1,2:T(8,128)(2,1)} %copy.38), kind=kOutput, calls=%fused_computation.46 | convolution fusion | flops 3221225472 | bytes 32505856 | tf_op jit(solution)/shard_map/rlk,mlkj->mrlj/dot_general | solution.py:40
  180.4 10.0 %fusion.19 = f32[8,1024,3,256]{3,1,2,0:T(8,128)} fusion(bf16[1024,8,256,1]{2,1,0,3:T(8,128)(2,1)S(1)} %bitcast.153, bf16[3,8,1,256,256]{4,3,2,1,0:T(8,128)(2,1)S(1)} %copy-done.8), kind=kOutput, calls=%fused_computation.37 | convolution fusion | flops 3221225472 | bytes 32505856 | tf_op jit(solution)/shard_map/rlk,mlkj->mrlj/dot_general | solution.py:29
  190.5 12.3 %fusion.28 = f32[8,3,256,1024]{2,3,1,0:T(8,128)} fusion(bf16[1024,8,256,1]{2,0,3,1:T(8,128)(2,1)S(1)} %bitcast.162, bf16[3,8,1,256,256]{3,4,0,1,2:T(8,128)(2,1)} %copy.35), kind=kOutput, calls=%fused_computation.48 | convolution fusion | flops 3221225472 | bytes 32505856 | tf_op jit(solution)/shard_map/rlk,mlkj->mrlj/dot_general | solution.py:40
  202.8 14.1 %fusion.17 = f32[8,3,256,1024]{2,3,1,0:T(8,128)} fusion(bf16[1024,8,256]{2,0,1:T(8,128)(2,1)} %collective-permute-done, bf16[3,8,1,256,256]{3,4,0,1,2:T(8,128)(2,1)S(1)} %copy-done.9), kind=kOutput, calls=%fused_computation.35 | convolution fusion | flops 3221225472 | bytes 32505856 | tf_op jit(solution)/shard_map/rlk,mlkj->mrlj/dot_general | solution.py:40
  216.9 45.5 %fusion.1 = bf16[3,1024,8,256]{3,1,0,2:T(8,128)(2,1)} fusion(f32[8,3,256,1024]{2,3,1,0:T(8,128)} %fusion.17, f32[8,3,256,1024]{2,3,1,0:T(8,128)} %fusion.24, f32[8,3,256,1024]{2,3,1,0:T(8,128)} %fusion.26, f32[8,3,256,1024]{2,3,1,0:T(8,128)} %fusion.28, f32[8,1024,3,256]{3,1,2,0:T(8,128)} %fusion.19, bf16[1024,8,256]{2,0,1:T(8,128)(2,1)} %collective-permute-done.1, ...), kind=kOutput, calls=%fused_computation.2 | convolution fusion | flops 3258974208 | bytes 145752064 | tf_op jit(solution)/shard_map/rlk,mlkj->mrlj/dot_general | solution.py:40
  262.4 7.5 %slice.41 = bf16[2,1024,8,256]{3,1,0,2:T(8,128)(2,1)} slice(bf16[3,1024,8,256]{3,1,0,2:T(8,128)(2,1)} %fusion.1), slice={[1:3], [0:1024], [0:8], [0:256]} | slice | bytes 16777216 | tf_op jit(solution)/shard_map/slice | solution.py:59
  269.9 11.4 %copy.50 = bf16[2,1024,8,256]{3,2,1,0:T(8,128)(2,1)} copy(bf16[2,1024,8,256]{3,1,0,2:T(8,128)(2,1)} %slice.41) | data formatting | bytes 16777216 | tf_op jit(solution)/shard_map/slice | solution.py:59
  281.3 12.9 %slice.33 = bf16[2,4,256,16,128]{4,3,2,1,0:T(8,128)(2,1)} reshape(bf16[2,1024,8,256]{3,2,1,0:T(8,128)(2,1)} %copy.50) | data formatting | bytes 16777216 | tf_op jit(solution)/shard_map/slice | solution.py:59
  294.2 4.9 slice.42
  299.0 2.3 collective-permute-start.2
  303.6 4.4 copy.53
  307.9 7.1 %reshape_squeeze.6 = bf16[4,2,128,16,128]{4,3,2,1,0:T(8,128)(2,1)} reshape(bf16[1,1024,8,256]{3,2,1,0:T(8,128)(2,1)} %copy.53) | data formatting | bytes 8388608 | tf_op jit(solution)/shard_map/reshape;squeeze | solution.py:66
  315.0 34.1 %collective-permute-done.2 = bf16[2,4,128,16,128]{4,3,2,1,0:T(8,128)(2,1)} collective-permute-done((bf16[2,4,128,16,128]{4,3,2,1,0:T(8,128)(2,1)}, bf16[2,4,128,16,128]{4,3,2,1,0:T(8,128)(2,1)}, u32[]{:S(2)}, u32[]{:S(2)}) %collective-permute-start.2) | collective-permute-done | bytes 4194336 | tf_op jit(solution)/shard_map/ppermute | solution.py:20
  349.1 5.4 pad_maximum_fusion
  354.5 6.8 fusion.61
  361.3 9.1 %copy_dynamic-update-slice_fusion.1 = bf16[2,4,2,256,16,128]{5,3,4,2,1,0:T(8,128)(2,1)} fusion(bf16[2,4,2,128,16,128]{5,4,3,2,1,0:T(8,128)(2,1)} %get-tuple-element.17), kind=kLoop, calls=%fused_computation.23 | loop fusion | bytes 16777216
  370.4 9.1 %copy_dynamic-update-slice_fusion = bf16[2,4,2,256,16,128]{5,3,4,2,1,0:T(8,128)(2,1)} fusion(bf16[2,4,2,256,16,128]{5,3,4,2,1,0:T(8,128)(2,1)} %copy_dynamic-update-slice_fusion.1, bf16[2,4,2,128,16,128]{5,4,3,2,1,0:T(8,128)(2,1)} %get-tuple-element.16), kind=kLoop, calls=%fused_computation.22 | loop fusion | bytes 16777216 | tf_op jit(solution)/shard_map/concatenate | solution.py:65
  379.4 12.7 %fusion.6 = f32[4,2,16,128,256]{4,3,2,1,0:T(8,128)} fusion(bf16[2,4,2,256,16,128]{5,3,4,2,1,0:T(8,128)(2,1)} %copy_dynamic-update-slice_fusion, bf16[4,2,128,16,128]{4,3,2,1,0:T(8,128)(2,1)} %reshape_squeeze.6), kind=kOutput, calls=%fused_computation.19 | convolution fusion | flops 1073741824 | bytes 29360128 | tf_op jit(solution)/shard_map/scqhd,sckhd->schqk/dot_general | solution.py:67
  392.2 20.4 %fusion.62 = (f32[4,2,16,128]{3,2,1,0:T(8,128)S(1)}, f32[4,2,16,128,256]{4,3,2,1,0:T(8,128)}) fusion(f32[4,2,16,128,256]{4,3,2,1,0:T(8,128)} %fusion.6, pred[4,2,128,256]{3,2,1,0:T(8,128)(4,1)S(1)} %compare_and_fusion), kind=kOutput, calls=%fused_computation.99 | output fusion | flops 25166080 | bytes 33882112 | tf_op jit(solution)/shard_map/sub | solution.py:83
  412.6 12.4 %convert_bitcast_fusion = bf16[4,2,128,16,128]{2,4,3,1,0:T(8,128)(2,1)} fusion(f32[4,2,16,128,256]{4,3,2,1,0:T(8,128)} %get-tuple-element.19, f32[4,2,16,128]{3,2,1,0:T(8,128)S(1)} %get-tuple-element.18, bf16[2,4,2,256,16,128]{5,3,4,2,1,0:T(8,128)(2,1)} %copy_dynamic-update-slice_fusion), kind=kOutput, calls=%fused_computation.40 | convolution fusion | flops 1084227584 | bytes 29425664 | tf_op jit(solution)/shard_map/schqk,sckhd->scqhd/dot_general | solution.py:85
  425.0 7.8 %copy.56 = bf16[4,2,128,16,128]{4,3,2,1,0:T(8,128)(2,1)} copy(bf16[4,2,128,16,128]{2,4,3,1,0:T(8,128)(2,1)} %convert_bitcast_fusion) | data formatting | bytes 8388608 | tf_op jit(solution)/shard_map/convert_element_type | solution.py:86
  432.8 7.3 %reshape.171 = bf16[1024,8,256]{2,1,0:T(8,128)(2,1)} reshape(bf16[4,2,128,16,128]{4,3,2,1,0:T(8,128)(2,1)} %copy.56) | data formatting | bytes 8388608 | tf_op jit(solution)/shard_map/reshape | solution.py:86
  440.0 5.3 copy.58
  447.0 2.9 collective-permute-start.4
  449.9 3.1 copy.115
  453.1 7.6 %reshape_reshape.23 = bf16[1024,1,2,4,256]{4,3,2,0,1:T(4,128)(2,1)} reshape(bf16[4,2,128,16,128]{4,3,2,1,0:T(8,128)(2,1)} %copy.56) | data formatting | bytes 8388608 | tf_op jit(solution)/shard_map/reshape;reshape | solution.py:34
  460.7 7.6 %reshape_reshape.22 = bf16[1024,2,2,2,256]{4,3,2,1,0:T(2,128)(2,1)} reshape(bf16[4,2,128,16,128]{4,3,2,1,0:T(8,128)(2,1)} %copy.56) | data formatting | bytes 8388608 | tf_op jit(solution)/shard_map/reshape;reshape | solution.py:34
  468.3 7.6 %reshape_reshape.21 = bf16[1024,4,2,1,256]{4,2,1,0,3:T(2,128)(2,1)} reshape(bf16[4,2,128,16,128]{4,3,2,1,0:T(8,128)(2,1)} %copy.56) | data formatting | bytes 8388608 | tf_op jit(solution)/shard_map/reshape;reshape | solution.py:34
  476.0 5.6 rev.23
  481.5 5.0 copy.99
  486.5 7.0 %rev.22 = bf16[1024,2,2,2,256]{4,3,2,1,0:T(2,128)(2,1)} reverse(bf16[1024,2,2,2,256]{4,3,2,1,0:T(2,128)(2,1)} %reshape_reshape.22), dimensions={2} | reverse | bytes 8388608 | tf_op jit(solution)/shard_map/rev | solution.py:35
  493.5 5.0 copy.98
  498.5 38.1 %rev.21 = bf16[1024,4,2,1,256]{4,2,1,0,3:T(2,128)(2,1)} reverse(bf16[1024,4,2,1,256]{4,2,1,0,3:T(2,128)(2,1)} %reshape_reshape.21), dimensions={2} | reverse | bytes 8388608 | tf_op jit(solution)/shard_map/rev | solution.py:35
  536.7 3.2 copy.97
  541.4 4.5 fusion.37
  545.9 4.5 fusion.39
  550.3 4.5 fusion.41
  554.8 5.7 fusion.30
  560.5 66.3 %collective-permute-done.3 = bf16[1024,8,256]{2,0,1:T(8,128)(2,1)} collective-permute-done((bf16[1024,8,256]{2,0,1:T(8,128)(2,1)}, bf16[1024,8,256]{2,0,1:T(8,128)(2,1)}, u32[]{:S(2)}, u32[]{:S(2)}) %collective-permute-start.3) | collective-permute-done | bytes 4194336 | tf_op jit(solution)/shard_map/ppermute | solution.py:14
  626.8 6.8 fusion.35
  633.7 20.4 %fusion.12 = f32[1,1024,8,256]{3,1,2,0:T(8,128)} fusion(f32[8,256,1024]{1,2,0:T(8,128)} %fusion.35, f32[8,256,1024]{1,2,0:T(8,128)} %fusion.37, f32[8,256,1024]{1,2,0:T(8,128)} %fusion.39, f32[8,256,1024]{1,2,0:T(8,128)} %fusion.41, f32[8,1024,256]{2,1,0:T(8,128)} %fusion.30, bf16[1024,8,256]{2,0,1:T(8,128)(2,1)} %collective-permute-done.4, ...), kind=kOutput, calls=%fused_computation.29 | convolution fusion | flops 1084227584 | bytes 55574532 | tf_op jit(solution)/shard_map/rlk,mlkj->mrlj/dot_general | solution.py:40
  654.1 11.7 %copy.77 = f32[1,1024,8,256]{3,2,1,0:T(8,128)} copy(f32[1,1024,8,256]{3,1,2,0:T(8,128)} %fusion.12) | data formatting | bytes 16777216 | tf_op jit(solution)/shard_map/add | solution.py:40
  665.8 9.2 %reshape_squeeze.7 = f32[4,256,2048]{2,1,0:T(8,128)} reshape(f32[1,1024,8,256]{3,2,1,0:T(8,128)} %copy.77) | data formatting | bytes 16777216 | tf_op jit(solution)/shard_map/reshape;squeeze | solution.py:88
  675.0 10.1 %convert_add_fusion = f32[4,256,2048]{2,1,0:T(8,128)} fusion(f32[4,256,2048]{2,1,0:T(8,128)} %reshape_squeeze.7, bf16[4,256,2048]{2,1,0:T(8,128)(2,1)} %param.6), kind=kLoop, calls=%fused_computation.12 | loop fusion | flops 4194304 | bytes 20971520 | tf_op jit(solution)/shard_map/add | solution.py:88
  (55 shorter events, 8.1 us)
Async XLA Ops:
  18.3 4.8 copy-start
  19.9 3.3 copy-start.2
  19.9 3.6 copy-start.12
  23.1 179.6 %collective-permute-start = (bf16[1024,8,256]{2,0,1:T(8,128)(2,1)}, bf16[1024,8,256]{2,0,1:T(8,128)(2,1)}, u32[]{:S(2)}, u32[]{:S(2)}) collective-permute-start(bf16[1024,8,256]{2,0,1:T(8,128)(2,1)} %copy.45), channel_id=1, source_target_pairs={{0,1},{1,0},{2,3},{3,2},{4,5},{5,4},{6,7},{7,6},{8,9},{9,8},{10,11... | collective-permute-start | bytes 12582920 | tf_op jit(solution)/shard_map/ppermute | solution.py:14
  23.1 193.7 %collective-permute-start.1 = (bf16[1024,8,256]{2,0,1:T(8,128)(2,1)}, bf16[1024,8,256]{2,0,1:T(8,128)(2,1)}, u32[]{:S(2)}, u32[]{:S(2)}) collective-permute-start(bf16[1024,8,256]{2,0,1:T(8,128)(2,1)} %copy.45), channel_id=1, source_target_pairs={{0,2},{1,3},{2,0},{3,1},{4,6},{5,7},{6,4},{7,5},{8,10},{9,11},{10,... | collective-permute-start | bytes 12582920 | tf_op jit(solution)/shard_map/ppermute | solution.py:14
  153.2 15.1 %copy-start.7 = (bf16[1024,2,2,2,256]{4,0,3,2,1:T(8,128)(2,1)S(1)}, bf16[1024,2,2,2,256]{4,0,3,2,1:T(8,128)(2,1)}, u32[]{:S(2)}) copy-start(bf16[1024,2,2,2,256]{4,0,3,2,1:T(8,128)(2,1)} %copy.39) | copy-start | bytes 12582916
  168.3 12.1 %copy-start.3 = (bf16[128,8,8,256]{3,2,1,0:T(8,128)(2,1)S(1)}, bf16[128,8,8,256]{3,2,1,0:T(8,128)(2,1)}, u32[]{:S(2)}) copy-start(bf16[128,8,8,256]{3,2,1,0:T(8,128)(2,1)} %copy-done.2) | copy-start | bytes 12582916
  168.3 12.1 %copy-start.8 = (bf16[3,8,1,256,256]{4,3,2,1,0:T(8,128)(2,1)S(1)}, bf16[3,8,1,256,256]{4,3,2,1,0:T(8,128)(2,1)}, u32[]{:S(2)}) copy-start(bf16[3,8,1,256,256]{4,3,2,1,0:T(8,128)(2,1)} %get-tuple-element.14) | copy-start | bytes 9437188
  180.4 10.1 %copy-start.6 = (bf16[1024,4,2,1,256]{4,0,2,1,3:T(8,128)(2,1)S(1)}, bf16[1024,4,2,1,256]{4,0,2,1,3:T(8,128)(2,1)}, u32[]{:S(2)}) copy-start(bf16[1024,4,2,1,256]{4,0,2,1,3:T(8,128)(2,1)} %copy.36) | copy-start | bytes 12582916
  190.5 12.3 %copy-start.9 = (bf16[3,8,1,256,256]{3,4,0,1,2:T(8,128)(2,1)S(1)}, bf16[3,8,1,256,256]{3,4,0,1,2:T(8,128)(2,1)}, u32[]{:S(2)}) copy-start(bf16[3,8,1,256,256]{3,4,0,1,2:T(8,128)(2,1)} %copy.44) | copy-start | bytes 9437188
  202.7 14.2 %copy-start.10 = (bf16[3,8,1,256,256]{3,4,0,1,2:T(8,128)(2,1)S(1)}, bf16[3,8,1,256,256]{3,4,0,1,2:T(8,128)(2,1)}, u32[]{:S(2)}) copy-start(bf16[3,8,1,256,256]{3,4,0,1,2:T(8,128)(2,1)} %copy.47) | copy-start | bytes 9437188
  294.2 7.2 %copy-start.11 = (s32[4,256]{1,0:T(4,128)S(1)}, s32[4,256]{1,0:T(4,128)}, u32[]{:S(2)}) copy-start(s32[4,256]{1,0:T(4,128)} %param.11) | copy-start | bytes 12292
  299.0 50.1 %collective-permute-start.2 = (bf16[2,4,128,16,128]{4,3,2,1,0:T(8,128)(2,1)}, bf16[2,4,128,16,128]{4,3,2,1,0:T(8,128)(2,1)}, u32[]{:S(2)}, u32[]{:S(2)}) collective-permute-start(bf16[2,4,128,16,128]{4,3,2,1,0:T(8,128)(2,1)} %slice.42), channel_id=1, source_target_pairs={{0,4},{4,8},{8,12},{12,16},{16,20},{20,24},{24,28},{1,5},{5,9},{9,... | collective-permute-start | bytes 12582920 | tf_op jit(solution)/shard_map/ppermute | solution.py:20
  301.4 2.2 slice-start
  432.8 17.2 %slice-start.1 = ((s8[6291456]{0:T(1024)(128)(4,1)}), s8[2097152]{0:T(1024)(128)(4,1)S(1)}, s32[]{:S(2)}) async-start(s8[6291456]{0:T(1024)(128)(4,1)} %bitcast.154), calls=%async_computation.1 | async-start | bytes 4194304
  440.0 9.9 %slice-start.2 = ((s8[6291456]{0:T(1024)(128)(4,1)}), s8[4194304]{0:T(1024)(128)(4,1)S(1)}, s32[]{:S(2)}) async-start(s8[6291456]{0:T(1024)(128)(4,1)} %bitcast.154), calls=%async_computation.2 | async-start | bytes 8388608
  445.3 181.5 %collective-permute-start.3 = (bf16[1024,8,256]{2,0,1:T(8,128)(2,1)}, bf16[1024,8,256]{2,0,1:T(8,128)(2,1)}, u32[]{:S(2)}, u32[]{:S(2)}) collective-permute-start(bf16[1024,8,256]{2,0,1:T(8,128)(2,1)} %copy.58), channel_id=1, source_target_pairs={{0,1},{1,0},{2,3},{3,2},{4,5},{5,4},{6,7},{7,6},{8,9},{9,8},{10,11... | collective-permute-start | bytes 12582920 | tf_op jit(solution)/shard_map/ppermute | solution.py:14
  447.0 186.7 %collective-permute-start.4 = (bf16[1024,8,256]{2,0,1:T(8,128)(2,1)}, bf16[1024,8,256]{2,0,1:T(8,128)(2,1)}, u32[]{:S(2)}, u32[]{:S(2)}) collective-permute-start(bf16[1024,8,256]{2,0,1:T(8,128)(2,1)} %copy.58), channel_id=1, source_target_pairs={{0,2},{1,3},{2,0},{3,1},{4,6},{5,7},{6,4},{7,5},{8,10},{9,11},{10,... | collective-permute-start | bytes 12582920 | tf_op jit(solution)/shard_map/ppermute | solution.py:14
  498.5 41.3 %slice-start.3 = ((s8[6291456]{0:T(1024)(128)(4,1)}), s8[2097152]{0:T(1024)(128)(4,1)S(1)}, s32[]{:S(2)}) async-start(s8[6291456]{0:T(1024)(128)(4,1)} %bitcast.156), calls=%async_computation.3 | async-start | bytes 4194304
  536.6 3.5 slice-start.4
  536.6 4.7 copy-start.4
  541.4 4.5 copy-start.5
  550.3 4.5 copy-start.1
where the time goes:
time: 698 us; the launch traced here: 686 us
  local copies, waits for them, and re-layouts  335 us (48%)
  matrix products  181 us (26%)
  waiting for transfers between devices  100 us (14%)
  other arithmetic  43.5 us (6%)
  blocking collectives  12 us (2%)
  starting transfers between devices  7.26 us (1%)
    dot_general x10, matrix products, butterfly(): jnp.einsum('rlk,mlkj->mrlj', partner, chosen, preferred_element_type=jnp....  140 us
    rev x9, local copies, waits for them, and re-layouts, butterfly(): partner = split[:, :, ::-1].reshape(rows, local_blocks, block)  116 us
    ppermute x4, waiting for transfers between devices, swapped(): return lax.ppermute(value, axis, pairs)  66.3 us
    another operation x6, local copies, waits for them, and re-layouts, butterfly(): split = blocks.reshape(rows, local_blocks // (2 << bit), 2, 1 << bit, block)  46.5 us
    ppermute x1, waiting for transfers between devices, passed_along(): return lax.ppermute(shard, axis, pairs)  34.1 us
    dynamic_slice x6, local copies, waits for them, and re-layouts, butterfly(): chosen = lax.dynamic_index_in_dim(weight, section, axis=2, keepdims=False)  33.9 us
    slice x3, local copies, waits for them, and re-layouts, per_device(): key_value = projected[1:3]  31.8 us
    sub x1, other arithmetic, per_device(): expo = jnp.exp(masked - top)  20.4 us
  transfers between devices with their start and end apart: 5, of which 2 were waited for; matrix products, arithmetic and copies ran while one was open for 46% of the time, Pallas kernels for 0%

commit v1 on v0

v1 whole, which is shorter than its diff:
```python
import functools

import jax
import jax.numpy as jnp
from jax import lax
from jax.experimental import pallas as pl
from jax.experimental.pallas import tpu as pltpu
from jax.sharding import PartitionSpec as P

D = 8192
WINDOW = 128
HEAD = 128
VMEM_LIMIT = 48 * 2**20


def swapped(value, axis, bit):
    mask = 2**bit
    pairs = [(source, source ^ mask) for source in range(lax.axis_size(axis))]
    return lax.ppermute(value, axis, pairs)


def passed_along(shard, axis, by):
    devices = lax.axis_size(axis)
    pairs = [(i, i + by) for i in range(devices) if 0 <= i + by < devices]
    return lax.ppermute(shard, axis, pairs)


def params():
    return pltpu.CompilerParams(
        dimension_semantics=("arbitrary",), vmem_limit_bytes=VMEM_LIMIT
    )


def partner_slots(bits_ref, i, local_blocks, sections):
    local_bits = local_blocks.bit_length() - 1
    slots = [i]
    for s in range(sections):
        bit = bits_ref[s]
        near = lax.bitwise_xor(i, lax.shift_left(jnp.int32(1), bit))
        far = (1 + bit - local_bits) * local_blocks + i
        slots.append(jnp.where(bit < local_bits, near, far))
    return slots


def stage_kernel(x_ref, *rest):
    rest[-1][...] = x_ref[0]


def stage(tokens, s, after):
    seqs, rows, width = tokens.shape
    return pl.pallas_call(
        stage_kernel,
        grid=(1,),
        in_specs=[pl.BlockSpec((1, rows, width), lambda i: (s, 0, 0))]
        + [pl.BlockSpec(memory_space=pl.ANY)] * len(after),
        out_specs=pl.BlockSpec((rows, width), lambda i: (0, 0)),
        out_shape=jax.ShapeDtypeStruct((rows, width), tokens.dtype),
        compiler_params=params(),
        cost_estimate=pl.CostEstimate(
            flops=0, bytes_accessed=4 * rows * width, transcendentals=0
        ),
        name="stage",
    )(tokens, *after)


def qkv_kernel(parts, local_blocks, sections, bits_ref, *refs):
    x_refs = refs[:parts]
    scale_ref, gain_ref, w_ref, q_ref, kv_ref, tail_ref, normed = refs[parts:]
    i = pl.program_id(0)
    block = w_ref.shape[-1]

    @pl.when(i == 0)
    def _():
        scale = scale_ref[0]
        for part in range(parts):
            for b in range(local_blocks):
                lanes = slice(b * block, (b + 1) * block)
                x = x_refs[part][0, :, lanes] if part == 0 else x_refs[part][:, lanes]
                x = x.astype(jnp.float32) * scale * gain_ref[part : part + 1, lanes]
                normed[part * local_blocks + b] = x.astype(jnp.bfloat16)

    slots = partner_slots(bits_ref, i, local_blocks, sections)
    lhs = jnp.concatenate([normed[slot] for slot in slots], axis=1)
    rows = lhs.shape[0]
    for m in range(3):
        out = jnp.dot(lhs, w_ref[m, 0], preferred_element_type=jnp.float32)
        out = out.astype(jnp.bfloat16)
        if m == 0:
            q_ref[...] = out
        else:
            kv_ref[m - 1] = out
            tail_ref[m - 1] = out[rows - WINDOW :]


def project(section_bits, tokens, s, partners, scale, gains, weight):
    seqs, rows, width = tokens.shape
    _, local_blocks, depth, block = weight.shape
    sections = section_bits.shape[0]
    parts = 1 + len(partners)
    whole = lambda i, bits: (0, 0)
    bf16 = jnp.bfloat16
    return pl.pallas_call(
        functools.partial(qkv_kernel, parts, local_blocks, sections),
        grid_spec=pltpu.PrefetchScalarGridSpec(
            num_scalar_prefetch=1,
            grid=(local_blocks,),
            in_specs=[pl.BlockSpec((1, rows, width), lambda i, bits: (s, 0, 0))]
            + [pl.BlockSpec((rows, width), whole)] * len(partners)
            + [
                pl.BlockSpec((1, rows, 1), lambda i, bits: (s, 0, 0)),
                pl.BlockSpec((parts, width), whole),
                pl.BlockSpec((3, 1, depth, block), lambda i, bits: (0, i, 0, 0)),
            ],
            out_specs=[
                pl.BlockSpec((rows, block), lambda i, bits: (0, i)),
                pl.BlockSpec((2, rows, block), lambda i, bits: (0, 0, i)),
                pl.BlockSpec((2, WINDOW, block), lambda i, bits: (0, 0, i)),
            ],
            scratch_shapes=[pltpu.VMEM((parts * local_blocks, rows, block), bf16)],
        ),
        out_shape=[
            jax.ShapeDtypeStruct((rows, width), bf16),
            jax.ShapeDtypeStruct((2, rows, width), bf16),
            jax.ShapeDtypeStruct((2, WINDOW, width), bf16),
        ],
        compiler_params=params(),
        cost_estimate=pl.CostEstimate(
            flops=6 * rows * depth * width,
            bytes_accessed=2 * weight.size + 2 * rows * width * (parts + 4),
            transcendentals=0,
        ),
        name="project",
    )(section_bits, tokens, *partners, scale, gains, weight)


def attend_kernel(q_ref, kv_ref, rim_ref, reach_ref, out_ref):
    rows, width = q_ref.shape
    for c in range(rows // WINDOW):
        here = slice(c * WINDOW, (c + 1) * WINDOW)
        row = lax.broadcasted_iota(jnp.int32, (WINDOW, 2 * WINDOW), 0)
        col = lax.broadcasted_iota(jnp.int32, (WINDOW, 2 * WINDOW), 1)
        dist = row + WINDOW - col
        valid = (dist >= 0) & (dist <= reach_ref[0, here])
        for h in range(width // HEAD):
            lanes = slice(h * HEAD, (h + 1) * HEAD)
            near = []
            for m in range(2):
                if c == 0:
                    before = rim_ref[m, :, lanes]
                else:
                    before = kv_ref[m, (c - 1) * WINDOW : c * WINDOW, lanes]
                near.append(jnp.concatenate([before, kv_ref[m, here, lanes]], axis=0))
            scores = lax.dot_general(
                q_ref[here, lanes],
                near[0],
                (((1,), (1,)), ((), ())),
                preferred_element_type=jnp.float32,
            )
            masked = jnp.where(valid, scores * HEAD ** (-0.5), -1e30)
            top = jnp.max(masked, axis=-1, keepdims=True)
            expo = jnp.exp(masked - top)
            total = jnp.sum(expo, axis=-1, keepdims=True)
            weights = (expo * (1.0 / total)).astype(jnp.bfloat16)
            mixed = jnp.dot(weights, near[1], preferred_element_type=jnp.float32)
            out_ref[here, lanes] = mixed.astype(jnp.bfloat16)


def attend(q, kv, rim, reach, s):
    rows, width = q.shape
    step = min(width, 4 * HEAD)
    return pl.pallas_call(
        attend_kernel,
        grid=(width // step,),
        in_specs=[
            pl.BlockSpec((rows, step), lambda i: (0, i)),
            pl.BlockSpec((2, rows, step), lambda i: (0, 0, i)),
            pl.BlockSpec((2, WINDOW, step), lambda i: (0, 0, i)),
            pl.BlockSpec((1, rows, 1), lambda i: (s, 0, 0)),
        ],
        out_specs=pl.BlockSpec((rows, step), lambda i: (0, i)),
        out_shape=jax.ShapeDtypeStruct((rows, width), jnp.bfloat16),
        compiler_params=params(),
        cost_estimate=pl.CostEstimate(
            flops=8 * rows * WINDOW * width,
            bytes_accessed=2 * rows * width * 5,
            transcendentals=2 * rows * WINDOW * (width // HEAD),
        ),
        name="attend",
    )(q, kv, rim, reach)


def out_kernel(parts, local_blocks, sections, bits_ref, *refs):
    a_refs = refs[:parts]
    x_ref, w_ref = refs[parts : parts + 2]
    out_ref, gathered = refs[-2:]
    i = pl.program_id(0)
    block = w_ref.shape[-1]

    @pl.when(i == 0)
    def _():
        for part in range(parts):
            for b in range(local_blocks):
                lanes = slice(b * block, (b + 1) * block)
                gathered[part * local_blocks + b] = a_refs[part][:, lanes]

    slots = partner_slots(bits_ref, i, local_blocks, sections)
    lhs = jnp.concatenate([gathered[slot] for slot in slots], axis=1)
    out = jnp.dot(lhs, w_ref[0], preferred_element_type=jnp.float32)
    out_ref[0] = x_ref[0].astype(jnp.float32) + out


def finish(section_bits, blocks, tokens, s, weight, result):
    seqs, rows, width = tokens.shape
    local_blocks, depth, block = weight.shape
    sections = section_bits.shape[0]
    parts = len(blocks)
    one = lambda i, bits: (s, 0, i)
    earlier = [] if result is None else [result]
    return pl.pallas_call(
        functools.partial(out_kernel, parts, local_blocks, sections),
        grid_spec=pltpu.PrefetchScalarGridSpec(
            num_scalar_prefetch=1,
            grid=(local_blocks,),
            in_specs=[pl.BlockSpec((rows, width), lambda i, bits: (0, 0))] * parts
            + [
                pl.BlockSpec((1, rows, block), one),
                pl.BlockSpec((1, depth, block), lambda i, bits: (i, 0, 0)),
            ]
            + [pl.BlockSpec(memory_space=pl.ANY)] * len(earlier),
            out_specs=pl.BlockSpec((1, rows, block), one),
            scratch_shapes=[
                pltpu.VMEM((parts * local_blocks, rows, block), jnp.bfloat16)
            ],
        ),
        out_shape=jax.ShapeDtypeStruct(tokens.shape, jnp.float32),
        input_output_aliases={} if result is None else {3 + parts: 0},
        compiler_params=params(),
        cost_estimate=pl.CostEstimate(
            flops=2 * rows * depth * width,
            bytes_accessed=2 * weight.size + rows * width * (2 * parts + 6),
            transcendentals=0,
        ),
        name="finish",
    )(section_bits, *blocks, tokens, weight, *earlier)


def per_device(tokens, norm_gain, qkv_weight, out_weight, section_bits, positions):
    seqs, rows, width = tokens.shape
    _, local_blocks, terms, block, _ = qkv_weight.shape
    device_bits = lax.axis_size("feat").bit_length() - 1
    far_first = list(range(device_bits))[::-1]
    qkv_weight = qkv_weight.reshape(3, local_blocks, terms * block, block)
    out_weight = out_weight.reshape(local_blocks, terms * block, block)

    def exchange(value):
        got = {bit: swapped(value, "feat", bit) for bit in far_first}
        return [got[bit] for bit in range(device_bits)]

    partners = []
    for s in range(seqs):
        partners.append(exchange(stage(tokens, s, partners[s - 2] if s >= 2 else [])))

    gains = jnp.stack([norm_gain] + exchange(norm_gain))
    x_full = tokens.astype(jnp.float32)
    row_squares = lax.psum(jnp.sum(x_full * x_full, axis=-1), "feat")
    scale = lax.rsqrt(row_squares / D + 1e-05)[..., None]
    index = lax.axis_index("ctx") * rows + jnp.arange(rows, dtype=jnp.int32)
    reach = jnp.minimum(jnp.minimum(positions, index), WINDOW - 1)[..., None]

    result = None
    blocks = []
    for s in range(seqs):
        q, kv, tail = project(
            section_bits, tokens, s, partners[s], scale, gains, qkv_weight
        )
        rim = passed_along(tail, "ctx", 1)
        attended = attend(q, kv, rim, reach, s)
        blocks.append([attended] + exchange(attended))
    for s in range(seqs):
        result = finish(section_bits, blocks[s], tokens, s, out_weight, result)
    return result


def solution(mesh):
    in_specs = (
        P(None, "ctx", "feat"),
        P("feat"),
        P(None, "feat", None, None, None),
        P("feat", None, None, None),
        P(),
        P(None, "ctx"),
    )
    out_specs = P(None, "ctx", "feat")
    return jax.shard_map(
        per_device, mesh=mesh, in_specs=in_specs, out_specs=out_specs, check_vma=False
    )
```

time: 698 us -> 428 us (0.61); the launches traced: 686 us -> 425 us
  local copies, waits for them, and re-layouts: 335 us -> 11.5 us
  matrix products: 181 us -> 0 us
  Pallas kernels: 0 us -> 124 us
  waiting for transfers between devices: 100 us -> 194 us
  blocking collectives: 12 us -> 68.1 us
  other arithmetic: 43.5 us -> 0.94 us
  starting transfers between devices: 7.26 us -> 26.4 us
    dot_general x14 -> x0, matrix products: 181 us -> none  [the longest x10 140 us: butterfly(): jnp.einsum('rlk,mlkj->mrlj', partner, chosen, preferred_element_type=jnp....]
    ppermute x4 -> x18, waiting for transfers between devices: 66.3 us -> 194 us  [swapped(): return lax.ppermute(value, axis, pairs)]
    pallas_call x0 -> x16, Pallas kernels: none -> 124 us  [the longest x4 59.6 us: project(): pl.pallas_call(functools.partial(qkv_kernel, parts, local_blocks, section...]
    rev x9 -> x0, local copies, waits for them, and re-layouts: 116 us -> none  [butterfly(): partner = split[:, :, ::-1].reshape(rows, local_blocks, block)]
    another operation x8 -> x0, local copies, waits for them, and re-layouts: 62.9 us -> none  [the longest x6 46.5 us: butterfly(): split = blocks.reshape(rows, local_blocks // (2 << bit), 2, 1 << bit, block)]
    psum x1, blocking collectives: 12 us -> 68.1 us  [per_device(): row_squares = lax.psum(jnp.sum(x_full * x_full, axis=-1), 'feat')]
    slice x8 -> x0, local copies, waits for them, and re-layouts: 49.4 us -> none  [the longest x3 31.8 us: per_device(): key_value = projected[1:3]]
    ppermute x1 -> x4, waiting for transfers between devices: 34.1 us -> 0.01 us  [passed_along(): return lax.ppermute(shard, axis, pairs)]
  transfers between devices with their start and end apart: 5 -> 22, of which waited for: 2 -> 9; matrix products, arithmetic and copies ran while one was open for 46% -> 0% of each run, Pallas kernels for 0% -> 27%
where the time goes in v1:
time: 428 us; the launch traced here: 425 us
  waiting for transfers between devices  194 us (45%)
  Pallas kernels  124 us (29%)
  blocking collectives  68.1 us (16%)
  starting transfers between devices  26.4 us (6%)
  local copies, waits for them, and re-layouts  11.5 us (3%)
    ppermute x18, waiting for transfers between devices, swapped(): return lax.ppermute(value, axis, pairs)  194 us
    psum x1, blocking collectives, per_device(): row_squares = lax.psum(jnp.sum(x_full * x_full, axis=-1), 'feat')  68.1 us
    pallas_call x4, Pallas kernels, project(): pl.pallas_call(functools.partial(qkv_kernel, parts, local_blocks, section...  59.6 us
    pallas_call x4, Pallas kernels, finish(): pl.pallas_call(functools.partial(out_kernel, parts, local_blocks, section...  35.7 us
    pallas_call x4, Pallas kernels, attend(): pl.pallas_call(attend_kernel, grid=(width // step,), in_specs=[pl.BlockSp...  21.8 us
    ppermute x18, starting transfers between devices, swapped(): return lax.ppermute(value, axis, pairs)  18 us
    unnamed x36, local copies, waits for them, and re-layouts  11 us
  transfers between devices with their start and end apart: 22, of which 9 were waited for; matrix products, arithmetic and copies ran while one was open for 0% of the time, Pallas kernels for 27%

profile of v1, /device:TPU:2, one launch (start us, length us, event | category | flops | bytes accessed | tf_op | source)
XLA Modules:
  0.0 425.5 jit_solution(13856703940560300417)
XLA Ops:
  0.0 2.2 copy-done
  2.2 1.0 stage.6
  3.2 2.6 collective-permute-start.10
  5.8 1.6 collective-permute-start.9
  7.4 0.4 collective-permute-start.4
  7.8 0.3 collective-permute-start.5
  8.2 1.1 stage.4
  9.2 1.6 collective-permute-start
  10.8 0.9 multiply_reduce_fusion
  11.7 68.1 %psum.7 = f32[4,256]{1,0:T(4,128)S(1)} all-reduce(f32[4,256]{1,0:T(4,128)S(1)} %multiply_reduce_fusion), channel_id=1, replica_groups=mesh['ctx'=8,'feat'=4] {'feat'}, use_global_device_ids=true, to_apply=%region_1.0 | all-reduce | flops 1024 | bytes 8192 | tf_op jit(solution)/shard_map/psum | solution.py:265
  79.9 0.2 copy.10.refs_3_
  80.1 0.1 collective-permute-start.1
  80.2 0.0 collective-permute-done.5
  80.2 0.0 collective-permute-done.10.rest_1_.refs_2_
  80.3 15.0 %project.7 = (bf16[256,2048]{1,0:T(8,128)(2,1)S(1)}, bf16[2,256,2048]{2,1,0:T(8,128)(2,1)}, bf16[2,128,2048]{2,1,0:T(8,128)(2,1)}) custom-call(s32[5]{0:T(128)S(1)} %copy-done.15, bf16[4,256,2048]{2,1,0:T(8,128)(2,1)} %refs_3_.7, bf16[256,2048]{1,0:T(8,128)(2,1)} %collective-permute-done.9.rest_0_.refs_1_, ...), custom_call_target="tpu_custom_call" | custom-call | flops 4831838208 | bytes 26214400 | tf_op jit(solution)/shard_map/project/pallas_call | solution.py:102
  95.2 1.0 copy-done.5
  96.2 2.0 collective-permute-start.19
  98.3 2.3 stage.7
  100.5 0.3 collective-permute-start.11
  100.8 2.6 collective-permute-start.12
  103.4 22.3 %collective-permute-done.1.rest_1_.refs_2_ = bf16[256,2048]{1,0:T(8,128)(2,1)S(1)} collective-permute-done((bf16[256,2048]{1,0:T(8,128)(2,1)}, bf16[256,2048]{1,0:T(8,128)(2,1)S(1)}, u32[]{:S(2)}, u32[]{:S(2)}) %collective-permute-start.1) | collective-permute-done | bytes 1048608 | tf_op jit(solution)/shard_map/ppermute | solution.py:19
  125.7 2.3 stage.5
  128.0 0.0 collective-permute-start.2
  128.0 2.9 collective-permute-start.3
  130.9 0.2 copy.11.reach_ref
  131.1 0.0 copy-start.1
  131.2 14.7 %project.6 = (bf16[256,2048]{1,0:T(8,128)(2,1)S(1)}, bf16[2,256,2048]{2,1,0:T(8,128)(2,1)}, bf16[2,128,2048]{2,1,0:T(8,128)(2,1)}) custom-call(s32[5]{0:T(128)S(1)} %copy-done.15, bf16[4,256,2048]{2,1,0:T(8,128)(2,1)} %refs_3_.7, bf16[256,2048]{1,0:T(8,128)(2,1)S(1)} %collective-permute-done.rest_0_.refs_1_, ...), custom_call_target="tpu_custom_call" | custom-call | flops 4831838208 | bytes 26214400 | tf_op jit(solution)/shard_map/project/pallas_call | solution.py:102
  145.8 1.9 collective-permute-start.16
  147.8 5.7 %attend.7.refs_0_ = bf16[256,2048]{1,0:T(8,128)(2,1)S(1)} custom-call(bf16[256,2048]{1,0:T(8,128)(2,1)S(1)} %copy-done.6, bf16[2,256,2048]{2,1,0:T(8,128)(2,1)S(1)} %copy-done.1, bf16[2,128,2048]{2,1,0:T(8,128)(2,1)} %collective-permute-done.19.rim_ref, s32[4,256,1]{2,1,0:T(8,128)S(1)} %copy.11.reach_ref), custom_call_target="tpu_custom_call" | custom-call | flops 536870912 | bytes 5242880 | tf_op jit(solution)/shard_map/attend/pallas_call | solution.py:171
  153.5 0.0 collective-permute-done.11.refs_1_
  153.5 0.1 collective-permute-start.20
  153.6 17.3 %collective-permute-done.12.refs_2_ = bf16[256,2048]{1,0:T(8,128)(2,1)} collective-permute-done((bf16[256,2048]{1,0:T(8,128)(2,1)}, bf16[256,2048]{1,0:T(8,128)(2,1)}, u32[]{:S(2)}, u32[]{:S(2)}) %collective-permute-start.12) | collective-permute-done | bytes 1048608 | tf_op jit(solution)/shard_map/ppermute | solution.py:19
  170.8 15.0 %project.5 = (bf16[256,2048]{1,0:T(8,128)(2,1)S(1)}, bf16[2,256,2048]{2,1,0:T(8,128)(2,1)}, bf16[2,128,2048]{2,1,0:T(8,128)(2,1)}) custom-call(s32[5]{0:T(128)S(1)} %copy-done.15, bf16[4,256,2048]{2,1,0:T(8,128)(2,1)} %refs_3_.7, bf16[256,2048]{1,0:T(8,128)(2,1)} %collective-permute-done.11.refs_1_, bf16[256,2048]{1,0:T(8,128)(2,1)} %collective-permute-done.12.refs_2_, ...), custom_call_target="tpu_custom_call" | custom-call | flops 4831838208 | bytes 26214400 | tf_op jit(solution)/shard_map/project/pallas_call | solution.py:102
  185.8 1.0 copy-done.11
  186.8 2.2 collective-permute-start.13
  189.0 8.0 %collective-permute-done.2.refs_1_ = bf16[256,2048]{1,0:T(8,128)(2,1)} collective-permute-done((bf16[256,2048]{1,0:T(8,128)(2,1)}, bf16[256,2048]{1,0:T(8,128)(2,1)}, u32[]{:S(2)}, u32[]{:S(2)}) %collective-permute-start.2) | collective-permute-done | bytes 1048608 | tf_op jit(solution)/shard_map/ppermute | solution.py:19
  197.0 18.8 %collective-permute-done.3.refs_2_ = bf16[256,2048]{1,0:T(8,128)(2,1)} collective-permute-done((bf16[256,2048]{1,0:T(8,128)(2,1)}, bf16[256,2048]{1,0:T(8,128)(2,1)}, u32[]{:S(2)}, u32[]{:S(2)}) %collective-permute-start.3) | collective-permute-done | bytes 1048608 | tf_op jit(solution)/shard_map/ppermute | solution.py:19
  215.7 15.0 %project.4 = (bf16[256,2048]{1,0:T(8,128)(2,1)S(1)}, bf16[2,256,2048]{2,1,0:T(8,128)(2,1)}, bf16[2,128,2048]{2,1,0:T(8,128)(2,1)}) custom-call(s32[5]{0:T(128)S(1)} %copy-done.15, bf16[4,256,2048]{2,1,0:T(8,128)(2,1)} %refs_3_.7, bf16[256,2048]{1,0:T(8,128)(2,1)} %collective-permute-done.2.refs_1_, bf16[256,2048]{1,0:T(8,128)(2,1)} %collective-permute-done.3.refs_2_, ...), custom_call_target="tpu_custom_call" | custom-call | flops 4831838208 | bytes 26214400 | tf_op jit(solution)/shard_map/project/pallas_call | solution.py:102
  230.7 1.0 copy-done.9
  231.7 2.2 collective-permute-start.6
  233.9 0.1 collective-permute-start.21
  234.0 0.0 collective-permute-done.16.rim_ref
  234.0 1.2 copy-done.8
  235.3 5.7 %attend.6.refs_0_ = bf16[256,2048]{1,0:T(8,128)(2,1)S(1)} custom-call(bf16[256,2048]{1,0:T(8,128)(2,1)S(1)} %copy-done.8, bf16[2,256,2048]{2,1,0:T(8,128)(2,1)S(1)} %copy-done.2, bf16[2,128,2048]{2,1,0:T(8,128)(2,1)} %collective-permute-done.16.rim_ref, s32[4,256,1]{2,1,0:T(8,128)S(1)} %copy.11.reach_ref), custom_call_target="tpu_custom_call" | custom-call | flops 536870912 | bytes 5242880 | tf_op jit(solution)/shard_map/attend/pallas_call | solution.py:171
  240.9 1.8 collective-permute-start.17
  242.8 1.2 collective-permute-start.18
  244.0 1.2 copy-done.12
  245.2 5.7 %attend.5.refs_0_ = bf16[256,2048]{1,0:T(8,128)(2,1)S(1)} custom-call(bf16[256,2048]{1,0:T(8,128)(2,1)S(1)} %copy-done.12, bf16[2,256,2048]{2,1,0:T(8,128)(2,1)S(1)} %copy-done.4, bf16[2,128,2048]{2,1,0:T(8,128)(2,1)} %collective-permute-done.13.rim_ref, s32[4,256,1]{2,1,0:T(8,128)S(1)} %copy.11.reach_ref), custom_call_target="tpu_custom_call" | custom-call | flops 536870912 | bytes 5242880 | tf_op jit(solution)/shard_map/attend/pallas_call | solution.py:171
  250.9 2.0 collective-permute-start.14
  252.9 1.0 copy-done.13
  253.9 0.0 collective-permute-start.15
  253.9 1.2 copy-done.10
  255.1 1.2 copy-done.14
  256.3 4.9 %attend.4.refs_0_ = bf16[256,2048]{1,0:T(8,128)(2,1)S(1)} custom-call(bf16[256,2048]{1,0:T(8,128)(2,1)S(1)} %copy-done.10, bf16[2,256,2048]{2,1,0:T(8,128)(2,1)S(1)} %copy-done.3, bf16[2,128,2048]{2,1,0:T(8,128)(2,1)S(1)} %copy-done.14, s32[4,256,1]{2,1,0:T(8,128)S(1)} %copy.11.reach_ref), custom_call_target="tpu_custom_call" | custom-call | flops 536870912 | bytes 5242880 | tf_op jit(solution)/shard_map/attend/pallas_call | solution.py:171
  261.2 21.3 %collective-permute-done.21.refs_2_ = bf16[256,2048]{1,0:T(8,128)(2,1)S(1)} collective-permute-done((bf16[256,2048]{1,0:T(8,128)(2,1)S(1)}, bf16[256,2048]{1,0:T(8,128)(2,1)S(1)}, u32[]{:S(2)}, u32[]{:S(2)}) %collective-permute-start.21) | collective-permute-done | bytes 1048608 | tf_op jit(solution)/shard_map/ppermute | solution.py:19
  282.5 6.4 %collective-permute-done.17.refs_1_ = bf16[256,2048]{1,0:T(8,128)(2,1)S(1)} collective-permute-done((bf16[256,2048]{1,0:T(8,128)(2,1)S(1)}, bf16[256,2048]{1,0:T(8,128)(2,1)S(1)}, u32[]{:S(2)}, u32[]{:S(2)}) %collective-permute-start.17) | collective-permute-done | bytes 1048608 | tf_op jit(solution)/shard_map/ppermute | solution.py:19
  288.9 0.4 collective-permute-start.8
  289.3 8.8 %finish.4.refs_5_ = f32[4,256,2048]{2,1,0:T(8,128)} custom-call(s32[5]{0:T(128)S(1)} %copy-done.15, bf16[256,2048]{1,0:T(8,128)(2,1)S(1)} %attend.7.refs_0_, bf16[256,2048]{1,0:T(8,128)(2,1)S(1)} %collective-permute-done.20.refs_1_, bf16[256,2048]{1,0:T(8,128)(2,1)S(1)} %collective-permute-done.21.refs_2_, bf16[4,256,2048]{2,1,0:T(8,128)(2,1)} %refs_3_.7, ...), custom_call_target="tpu_custom_call" | custom-call | flops 1610612736 | bytes 12582912 | tf_op jit(solution)/shard_map/finish/pallas_call | solution.py:219
  298.2 29.4 %collective-permute-done.18.refs_2_ = bf16[256,2048]{1,0:T(8,128)(2,1)} collective-permute-done((bf16[256,2048]{1,0:T(8,128)(2,1)S(1)}, bf16[256,2048]{1,0:T(8,128)(2,1)}, u32[]{:S(2)}, u32[]{:S(2)}) %collective-permute-start.18) | collective-permute-done | bytes 1048608 | tf_op jit(solution)/shard_map/ppermute | solution.py:19
  327.6 9.2 %finish.5.refs_5_ = f32[4,256,2048]{2,1,0:T(8,128)} custom-call(s32[5]{0:T(128)S(1)} %copy-done.15, bf16[256,2048]{1,0:T(8,128)(2,1)S(1)} %attend.6.refs_0_, bf16[256,2048]{1,0:T(8,128)(2,1)S(1)} %collective-permute-done.17.refs_1_, bf16[256,2048]{1,0:T(8,128)(2,1)} %collective-permute-done.18.refs_2_, ...), custom_call_target="tpu_custom_call", output_to_operand_aliasing={{}: (6, {})} | custom-call | flops 1610612736 | bytes 12582912 | tf_op jit(solution)/shard_map/finish/pallas_call | solution.py:219
  336.8 35.7 %collective-permute-done.15.refs_2_ = bf16[256,2048]{1,0:T(8,128)(2,1)S(1)} collective-permute-done((bf16[256,2048]{1,0:T(8,128)(2,1)S(1)}, bf16[256,2048]{1,0:T(8,128)(2,1)S(1)}, u32[]{:S(2)}, u32[]{:S(2)}) %collective-permute-start.15) | collective-permute-done | bytes 1048608 | tf_op jit(solution)/shard_map/ppermute | solution.py:19
  372.5 8.8 %finish.6.refs_5_ = f32[4,256,2048]{2,1,0:T(8,128)} custom-call(s32[5]{0:T(128)S(1)} %copy-done.15, bf16[256,2048]{1,0:T(8,128)(2,1)S(1)} %attend.5.refs_0_, bf16[256,2048]{1,0:T(8,128)(2,1)S(1)} %collective-permute-done.14.refs_1_, bf16[256,2048]{1,0:T(8,128)(2,1)S(1)} %collective-permute-done.15.refs_2_, ...), custom_call_target="tpu_custom_call", output_to_operand_aliasing={{}: (6, {})} | custom-call | flops 1610612736 | bytes 12582912 | tf_op jit(solution)/shard_map/finish/pallas_call | solution.py:219
  381.3 35.3 %collective-permute-done.8.refs_2_ = bf16[256,2048]{1,0:T(8,128)(2,1)S(1)} collective-permute-done((bf16[256,2048]{1,0:T(8,128)(2,1)S(1)}, bf16[256,2048]{1,0:T(8,128)(2,1)S(1)}, u32[]{:S(2)}, u32[]{:S(2)}) %collective-permute-start.8) | collective-permute-done | bytes 1048608 | tf_op jit(solution)/shard_map/ppermute | solution.py:19
  416.6 8.9 %finish.7 = f32[4,256,2048]{2,1,0:T(8,128)} custom-call(s32[5]{0:T(128)S(1)} %copy-done.15, bf16[256,2048]{1,0:T(8,128)(2,1)S(1)} %attend.4.refs_0_, bf16[256,2048]{1,0:T(8,128)(2,1)S(1)} %collective-permute-done.7.refs_1_, bf16[256,2048]{1,0:T(8,128)(2,1)S(1)} %collective-permute-done.8.refs_2_, ...), custom_call_target="tpu_custom_call", output_to_operand_aliasing={{}: (6, {})} | custom-call | flops 1610612736 | bytes 12582912 | tf_op jit(solution)/shard_map/finish/pallas_call | solution.py:219
  (40 shorter events, 0.1 us)
Async XLA Ops:
  0.0 2.2 copy-start
  2.2 78.0 %copy-start.16 = (f32[2048]{0:T(1024)S(1)}, f32[2048]{0:T(1024)}, u32[]{:S(2)}) copy-start(f32[2048]{0:T(1024)} %param.7) | copy-start | bytes 24580
  2.2 78.1 %copy-start.15 = (s32[5]{0:T(128)S(1)}, s32[5]{0:T(128)}, u32[]{:S(2)}) copy-start(s32[5]{0:T(128)} %bits_ref.15) | copy-start | bytes 64
  3.2 77.0 %collective-permute-start.10 = (bf16[256,2048]{1,0:T(8,128)(2,1)}, bf16[256,2048]{1,0:T(8,128)(2,1)}, u32[]{:S(2)}, u32[]{:S(2)}) collective-permute-start(bf16[256,2048]{1,0:T(8,128)(2,1)} %stage.6), channel_id=1, source_target_pairs={{0,2},{1,3},{2,0},{3,1},{4,6},{5,7},{6,4},{7,5},{8,10},{9,11},{10,... | collective-permute-start | bytes 3145736 | tf_op jit(solution)/shard_map/ppermute | solution.py:19
  5.8 74.4 %collective-permute-start.9 = (bf16[256,2048]{1,0:T(8,128)(2,1)}, bf16[256,2048]{1,0:T(8,128)(2,1)}, u32[]{:S(2)}, u32[]{:S(2)}) collective-permute-start(bf16[256,2048]{1,0:T(8,128)(2,1)} %stage.6), channel_id=1, source_target_pairs={{0,1},{1,0},{2,3},{3,2},{4,5},{5,4},{6,7},{7,6},{8,9},{9,8},{10,11... | collective-permute-start | bytes 3145736 | tf_op jit(solution)/shard_map/ppermute | solution.py:19
  7.4 72.7 %collective-permute-start.4 = (f32[2048]{0:T(1024)}, f32[2048]{0:T(1024)S(1)}, u32[]{:S(2)}, u32[]{:S(2)}) collective-permute-start(f32[2048]{0:T(1024)} %param.7), channel_id=1, source_target_pairs={{0,1},{1,0},{2,3},{3,2},{4,5},{5,4},{6,7},{7,6},{8,9},{9,8},{10,11... | collective-permute-start | bytes 24584 | tf_op jit(solution)/shard_map/ppermute | solution.py:19
  7.8 72.3 %collective-permute-start.5 = (f32[2048]{0:T(1024)}, f32[2048]{0:T(1024)S(1)}, u32[]{:S(2)}, u32[]{:S(2)}) collective-permute-start(f32[2048]{0:T(1024)} %param.7), channel_id=1, source_target_pairs={{0,2},{1,3},{2,0},{3,1},{4,6},{5,7},{6,4},{7,5},{8,10},{9,11},{10,... | collective-permute-start | bytes 24584 | tf_op jit(solution)/shard_map/ppermute | solution.py:19
  9.2 94.2 %collective-permute-start = (bf16[256,2048]{1,0:T(8,128)(2,1)}, bf16[256,2048]{1,0:T(8,128)(2,1)S(1)}, u32[]{:S(2)}, u32[]{:S(2)}) collective-permute-start(bf16[256,2048]{1,0:T(8,128)(2,1)} %stage.4), channel_id=1, source_target_pairs={{0,1},{1,0},{2,3},{3,2},{4,5},{5,4},{6,7},{7,6},{8,9},{9,8},{10,11... | collective-permute-start | bytes 3145736 | tf_op jit(solution)/shard_map/ppermute | solution.py:19
  80.1 45.6 %collective-permute-start.1 = (bf16[256,2048]{1,0:T(8,128)(2,1)}, bf16[256,2048]{1,0:T(8,128)(2,1)S(1)}, u32[]{:S(2)}, u32[]{:S(2)}) collective-permute-start(bf16[256,2048]{1,0:T(8,128)(2,1)} %stage.4), channel_id=1, source_target_pairs={{0,2},{1,3},{2,0},{3,1},{4,6},{5,7},{6,4},{7,5},{8,10},{9,11},{10,... | collective-permute-start | bytes 3145736 | tf_op jit(solution)/shard_map/ppermute | solution.py:19
  95.2 1.0 copy-start.5
  96.2 34.7 %copy-start.17 = (s32[4,256]{1,0:T(4,128)S(1)}, s32[4,256]{1,0:T(4,128)}, u32[]{:S(2)}) copy-start(s32[4,256]{1,0:T(4,128)} %param.11) | copy-start | bytes 12292
  96.2 49.6 %collective-permute-start.19 = (bf16[2,128,2048]{2,1,0:T(8,128)(2,1)}, bf16[2,128,2048]{2,1,0:T(8,128)(2,1)}, u32[]{:S(2)}, u32[]{:S(2)}) collective-permute-start(bf16[2,128,2048]{2,1,0:T(8,128)(2,1)} %get-tuple-element.28), channel_id=1, source_target_pairs={{0,4},{4,8},{8,12},{12,16},{16,20},{20,24},{24,28},{1,5},{5,9},{9,... | collective-permute-start | bytes 3145736 | tf_op jit(solution)/shard_map/ppermute | solution.py:25
  100.5 52.9 %collective-permute-start.11 = (bf16[256,2048]{1,0:T(8,128)(2,1)}, bf16[256,2048]{1,0:T(8,128)(2,1)}, u32[]{:S(2)}, u32[]{:S(2)}) collective-permute-start(bf16[256,2048]{1,0:T(8,128)(2,1)} %stage.7), channel_id=1, source_target_pairs={{0,1},{1,0},{2,3},{3,2},{4,5},{5,4},{6,7},{7,6},{8,9},{9,8},{10,11... | collective-permute-start | bytes 3145736 | tf_op jit(solution)/shard_map/ppermute | solution.py:19
  100.8 70.0 %collective-permute-start.12 = (bf16[256,2048]{1,0:T(8,128)(2,1)}, bf16[256,2048]{1,0:T(8,128)(2,1)}, u32[]{:S(2)}, u32[]{:S(2)}) collective-permute-start(bf16[256,2048]{1,0:T(8,128)(2,1)} %stage.7), channel_id=1, source_target_pairs={{0,2},{1,3},{2,0},{3,1},{4,6},{5,7},{6,4},{7,5},{8,10},{9,11},{10,... | collective-permute-start | bytes 3145736 | tf_op jit(solution)/shard_map/ppermute | solution.py:19
  128.0 69.0 %collective-permute-start.2 = (bf16[256,2048]{1,0:T(8,128)(2,1)}, bf16[256,2048]{1,0:T(8,128)(2,1)}, u32[]{:S(2)}, u32[]{:S(2)}) collective-permute-start(bf16[256,2048]{1,0:T(8,128)(2,1)} %stage.5), channel_id=1, source_target_pairs={{0,1},{1,0},{2,3},{3,2},{4,5},{5,4},{6,7},{7,6},{8,9},{9,8},{10,11... | collective-permute-start | bytes 3145736 | tf_op jit(solution)/shard_map/ppermute | solution.py:19
  128.0 87.7 %collective-permute-start.3 = (bf16[256,2048]{1,0:T(8,128)(2,1)}, bf16[256,2048]{1,0:T(8,128)(2,1)}, u32[]{:S(2)}, u32[]{:S(2)}) collective-permute-start(bf16[256,2048]{1,0:T(8,128)(2,1)} %stage.5), channel_id=1, source_target_pairs={{0,2},{1,3},{2,0},{3,1},{4,6},{5,7},{6,4},{7,5},{8,10},{9,11},{10,... | collective-permute-start | bytes 3145736 | tf_op jit(solution)/shard_map/ppermute | solution.py:19
  131.1 16.6 %copy-start.1 = (bf16[2,256,2048]{2,1,0:T(8,128)(2,1)S(1)}, bf16[2,256,2048]{2,1,0:T(8,128)(2,1)}, u32[]{:S(2)}) copy-start(bf16[2,256,2048]{2,1,0:T(8,128)(2,1)} %get-tuple-element.27.kv_ref) | copy-start | bytes 6291460
  131.2 16.6 %copy-start.6 = (bf16[256,2048]{1,0:T(8,128)(2,1)S(1)}, bf16[256,2048]{1,0:T(8,128)(2,1)}, u32[]{:S(2)}) copy-start(bf16[256,2048]{1,0:T(8,128)(2,1)} %copy-done.5) | copy-start | bytes 3145732
  145.8 7.6 %copy-start.7 = (bf16[256,2048]{1,0:T(8,128)(2,1)}, bf16[256,2048]{1,0:T(8,128)(2,1)S(1)}, u32[]{:S(2)}) copy-start(bf16[256,2048]{1,0:T(8,128)(2,1)S(1)} %get-tuple-element.23.q_ref) | copy-start | bytes 3145732
  145.8 88.2 %collective-permute-start.16 = (bf16[2,128,2048]{2,1,0:T(8,128)(2,1)}, bf16[2,128,2048]{2,1,0:T(8,128)(2,1)}, u32[]{:S(2)}, u32[]{:S(2)}) collective-permute-start(bf16[2,128,2048]{2,1,0:T(8,128)(2,1)} %get-tuple-element.25), channel_id=1, source_target_pairs={{0,4},{4,8},{8,12},{12,16},{16,20},{20,24},{24,28},{1,5},{5,9},{9,... | collective-permute-start | bytes 3145736 | tf_op jit(solution)/shard_map/ppermute | solution.py:25
  153.5 97.4 %collective-permute-start.20 = (bf16[256,2048]{1,0:T(8,128)(2,1)S(1)}, bf16[256,2048]{1,0:T(8,128)(2,1)S(1)}, u32[]{:S(2)}, u32[]{:S(2)}) collective-permute-start(bf16[256,2048]{1,0:T(8,128)(2,1)S(1)} %attend.7.refs_0_), channel_id=1, source_target_pairs={{0,1},{1,0},{2,3},{3,2},{4,5},{5,4},{6,7},{7,6},{8,9},{9,8},{10,11... | collective-permute-start | bytes 3145736 | tf_op jit(solution)/shard_map/ppermute | solution.py:19
  185.8 1.0 copy-start.11
  186.8 47.2 %copy-start.2 = (bf16[2,256,2048]{2,1,0:T(8,128)(2,1)S(1)}, bf16[2,256,2048]{2,1,0:T(8,128)(2,1)}, u32[]{:S(2)}) copy-start(bf16[2,256,2048]{2,1,0:T(8,128)(2,1)} %get-tuple-element.24.kv_ref) | copy-start | bytes 6291460
  186.8 57.2 %copy-start.4 = (bf16[2,256,2048]{2,1,0:T(8,128)(2,1)S(1)}, bf16[2,256,2048]{2,1,0:T(8,128)(2,1)}, u32[]{:S(2)}) copy-start(bf16[2,256,2048]{2,1,0:T(8,128)(2,1)} %get-tuple-element.21.kv_ref) | copy-start | bytes 6291460
  186.8 56.0 %collective-permute-start.13 = (bf16[2,128,2048]{2,1,0:T(8,128)(2,1)}, bf16[2,128,2048]{2,1,0:T(8,128)(2,1)}, u32[]{:S(2)}, u32[]{:S(2)}) collective-permute-start(bf16[2,128,2048]{2,1,0:T(8,128)(2,1)} %get-tuple-element.22), channel_id=1, source_target_pairs={{0,4},{4,8},{8,12},{12,16},{16,20},{20,24},{24,28},{1,5},{5,9},{9,... | collective-permute-start | bytes 3145736 | tf_op jit(solution)/shard_map/ppermute | solution.py:25
  230.7 1.0 copy-start.9
  231.7 22.2 %copy-start.3 = (bf16[2,256,2048]{2,1,0:T(8,128)(2,1)S(1)}, bf16[2,256,2048]{2,1,0:T(8,128)(2,1)}, u32[]{:S(2)}) copy-start(bf16[2,256,2048]{2,1,0:T(8,128)(2,1)} %get-tuple-element.18.kv_ref) | copy-start | bytes 6291460
  231.7 21.2 %collective-permute-start.6 = (bf16[2,128,2048]{2,1,0:T(8,128)(2,1)}, bf16[2,128,2048]{2,1,0:T(8,128)(2,1)S(1)}, u32[]{:S(2)}, u32[]{:S(2)}) collective-permute-start(bf16[2,128,2048]{2,1,0:T(8,128)(2,1)} %get-tuple-element.19), channel_id=1, source_target_pairs={{0,4},{4,8},{8,12},{12,16},{16,20},{20,24},{24,28},{1,5},{5,9},{9,... | collective-permute-start | bytes 3145736 | tf_op jit(solution)/shard_map/ppermute | solution.py:25
  233.9 48.6 %collective-permute-start.21 = (bf16[256,2048]{1,0:T(8,128)(2,1)S(1)}, bf16[256,2048]{1,0:T(8,128)(2,1)S(1)}, u32[]{:S(2)}, u32[]{:S(2)}) collective-permute-start(bf16[256,2048]{1,0:T(8,128)(2,1)S(1)} %attend.7.refs_0_), channel_id=1, source_target_pairs={{0,2},{1,3},{2,0},{3,1},{4,6},{5,7},{6,4},{7,5},{8,10},{9,11},{10,... | collective-permute-start | bytes 3145736 | tf_op jit(solution)/shard_map/ppermute | solution.py:19
  234.0 1.2 copy-start.8
  240.9 48.0 %collective-permute-start.17 = (bf16[256,2048]{1,0:T(8,128)(2,1)S(1)}, bf16[256,2048]{1,0:T(8,128)(2,1)S(1)}, u32[]{:S(2)}, u32[]{:S(2)}) collective-permute-start(bf16[256,2048]{1,0:T(8,128)(2,1)S(1)} %attend.6.refs_0_), channel_id=1, source_target_pairs={{0,1},{1,0},{2,3},{3,2},{4,5},{5,4},{6,7},{7,6},{8,9},{9,8},{10,11... | collective-permute-start | bytes 3145736 | tf_op jit(solution)/shard_map/ppermute | solution.py:19
  242.8 84.9 %collective-permute-start.18 = (bf16[256,2048]{1,0:T(8,128)(2,1)S(1)}, bf16[256,2048]{1,0:T(8,128)(2,1)}, u32[]{:S(2)}, u32[]{:S(2)}) collective-permute-start(bf16[256,2048]{1,0:T(8,128)(2,1)S(1)} %attend.6.refs_0_), channel_id=1, source_target_pairs={{0,2},{1,3},{2,0},{3,1},{4,6},{5,7},{6,4},{7,5},{8,10},{9,11},{10,... | collective-permute-start | bytes 3145736 | tf_op jit(solution)/shard_map/ppermute | solution.py:19
  244.0 1.2 copy-start.12
  250.9 85.9 %collective-permute-start.14 = (bf16[256,2048]{1,0:T(8,128)(2,1)S(1)}, bf16[256,2048]{1,0:T(8,128)(2,1)S(1)}, u32[]{:S(2)}, u32[]{:S(2)}) collective-permute-start(bf16[256,2048]{1,0:T(8,128)(2,1)S(1)} %attend.5.refs_0_), channel_id=1, source_target_pairs={{0,1},{1,0},{2,3},{3,2},{4,5},{5,4},{6,7},{7,6},{8,9},{9,8},{10,11... | collective-permute-start | bytes 3145736 | tf_op jit(solution)/shard_map/ppermute | solution.py:19
  252.9 1.0 copy-start.13
  253.9 118.6 %collective-permute-start.15 = (bf16[256,2048]{1,0:T(8,128)(2,1)S(1)}, bf16[256,2048]{1,0:T(8,128)(2,1)S(1)}, u32[]{:S(2)}, u32[]{:S(2)}) collective-permute-start(bf16[256,2048]{1,0:T(8,128)(2,1)S(1)} %attend.5.refs_0_), channel_id=1, source_target_pairs={{0,2},{1,3},{2,0},{3,1},{4,6},{5,7},{6,4},{7,5},{8,10},{9,11},{10,... | collective-permute-start | bytes 3145736 | tf_op jit(solution)/shard_map/ppermute | solution.py:19
  253.9 1.2 copy-start.10
  255.1 1.2 copy-start.14
  282.5 98.8 %collective-permute-start.7 = (bf16[256,2048]{1,0:T(8,128)(2,1)S(1)}, bf16[256,2048]{1,0:T(8,128)(2,1)S(1)}, u32[]{:S(2)}, u32[]{:S(2)}) collective-permute-start(bf16[256,2048]{1,0:T(8,128)(2,1)S(1)} %attend.4.refs_0_), channel_id=1, source_target_pairs={{0,1},{1,0},{2,3},{3,2},{4,5},{5,4},{6,7},{7,6},{8,9},{9,8},{10,11... | collective-permute-start | bytes 3145736 | tf_op jit(solution)/shard_map/ppermute | solution.py:19
  288.9 127.7 %collective-permute-start.8 = (bf16[256,2048]{1,0:T(8,128)(2,1)S(1)}, bf16[256,2048]{1,0:T(8,128)(2,1)S(1)}, u32[]{:S(2)}, u32[]{:S(2)}) collective-permute-start(bf16[256,2048]{1,0:T(8,128)(2,1)S(1)} %attend.4.refs_0_), channel_id=1, source_target_pairs={{0,2},{1,3},{2,0},{3,1},{4,6},{5,7},{6,4},{7,5},{8,10},{9,11},{10,... | collective-permute-start | bytes 3145736 | tf_op jit(solution)/shard_map/ppermute | solution.py:19

commit v2 on v1

--- a/solution.py
+++ b/solution.py
@@ -65,7 +65,8 @@
 
 def qkv_kernel(parts, local_blocks, sections, bits_ref, *refs):
     x_refs = refs[:parts]
-    scale_ref, gain_ref, w_ref, q_ref, kv_ref, tail_ref, normed = refs[parts:]
+    scale_ref, gain_ref, w_ref = refs[parts : parts + 3]
+    q_ref, kv_ref, tail_ref, normed = refs[-4:]
     i = pl.program_id(0)
     block = w_ref.shape[-1]
 
@@ -92,7 +93,7 @@
             tail_ref[m - 1] = out[rows - WINDOW :]
 
 
-def project(section_bits, tokens, s, partners, scale, gains, weight):
+def project(section_bits, tokens, s, partners, scale, gains, weight, after):
     seqs, rows, width = tokens.shape
     _, local_blocks, depth, block = weight.shape
     sections = section_bits.shape[0]
@@ -110,7 +111,8 @@
                 pl.BlockSpec((1, rows, 1), lambda i, bits: (s, 0, 0)),
                 pl.BlockSpec((parts, width), whole),
                 pl.BlockSpec((3, 1, depth, block), lambda i, bits: (0, i, 0, 0)),
-            ],
+            ]
+            + [pl.BlockSpec(memory_space=pl.ANY)] * len(after),
             out_specs=[
                 pl.BlockSpec((rows, block), lambda i, bits: (0, i)),
                 pl.BlockSpec((2, rows, block), lambda i, bits: (0, 0, i)),
@@ -130,10 +132,11 @@
             transcendentals=0,
         ),
         name="project",
-    )(section_bits, tokens, *partners, scale, gains, weight)
-
-
-def attend_kernel(q_ref, kv_ref, rim_ref, reach_ref, out_ref):
+    )(section_bits, tokens, *partners, scale, gains, weight, *after)
+
+
+def attend_kernel(q_ref, kv_ref, rim_ref, reach_ref, *rest):
+    out_ref = rest[-1]
     rows, width = q_ref.shape
     for c in range(rows // WINDOW):
         here = slice(c * WINDOW, (c + 1) * WINDOW)
@@ -165,7 +168,7 @@
             out_ref[here, lanes] = mixed.astype(jnp.bfloat16)
 
 
-def attend(q, kv, rim, reach, s):
+def attend(q, kv, rim, reach, s, after):
     rows, width = q.shape
     step = min(width, 4 * HEAD)
     return pl.pallas_call(
@@ -176,7 +179,8 @@
             pl.BlockSpec((2, rows, step), lambda i: (0, 0, i)),
             pl.BlockSpec((2, WINDOW, step), lambda i: (0, 0, i)),
             pl.BlockSpec((1, rows, 1), lambda i: (s, 0, 0)),
-        ],
+        ]
+        + [pl.BlockSpec(memory_space=pl.ANY)] * len(after),
         out_specs=pl.BlockSpec((rows, step), lambda i: (0, i)),
         out_shape=jax.ShapeDtypeStruct((rows, width), jnp.bfloat16),
         compiler_params=params(),
@@ -186,7 +190,7 @@
             transcendentals=2 * rows * WINDOW * (width // HEAD),
         ),
         name="attend",
-    )(q, kv, rim, reach)
+    )(q, kv, rim, reach, *after)
 
 
 def out_kernel(parts, local_blocks, sections, bits_ref, *refs):
@@ -209,13 +213,13 @@
     out_ref[0] = x_ref[0].astype(jnp.float32) + out
 
 
-def finish(section_bits, blocks, tokens, s, weight, result):
+def finish(section_bits, blocks, tokens, s, weight, result, after):
     seqs, rows, width = tokens.shape
     local_blocks, depth, block = weight.shape
     sections = section_bits.shape[0]
     parts = len(blocks)
     one = lambda i, bits: (s, 0, i)
-    earlier = [] if result is None else [result]
+    earlier = ([] if result is None else [result]) + after
     return pl.pallas_call(
         functools.partial(out_kernel, parts, local_blocks, sections),
         grid_spec=pltpu.PrefetchScalarGridSpec(
@@ -256,28 +260,48 @@
         got = {bit: swapped(value, "feat", bit) for bit in far_first}
         return [got[bit] for bit in range(device_bits)]
 
-    partners = []
-    for s in range(seqs):
-        partners.append(exchange(stage(tokens, s, partners[s - 2] if s >= 2 else [])))
-
-    gains = jnp.stack([norm_gain] + exchange(norm_gain))
     x_full = tokens.astype(jnp.float32)
-    row_squares = lax.psum(jnp.sum(x_full * x_full, axis=-1), "feat")
-    scale = lax.rsqrt(row_squares / D + 1e-05)[..., None]
+    row_squares = jnp.sum(x_full * x_full, axis=-1).reshape(-1)
+    note = jnp.concatenate([row_squares, norm_gain])
+    notes = {}
+    for mask in range(1, lax.axis_size("feat")):
+        pairs = [(a, a ^ mask) for a in range(lax.axis_size("feat"))]
+        notes[mask] = lax.ppermute(note, "feat", pairs)
+    total = row_squares + sum(value[: seqs * rows] for value in notes.values())
+    scale = lax.rsqrt(total / D + 1e-05).reshape(seqs, rows, 1)
+    gains = jnp.stack(
+        [norm_gain] + [notes[1 << bit][seqs * rows :] for bit in range(device_bits)]
+    )
     index = lax.axis_index("ctx") * rows + jnp.arange(rows, dtype=jnp.int32)
     reach = jnp.minimum(jnp.minimum(positions, index), WINDOW - 1)[..., None]
 
+    ahead = 2
+    staged, partners, blocks, pending = {}, {}, {}, {}
     result = None
-    blocks = []
-    for s in range(seqs):
-        q, kv, tail = project(
-            section_bits, tokens, s, partners[s], scale, gains, qkv_weight
-        )
-        rim = passed_along(tail, "ctx", 1)
-        attended = attend(q, kv, rim, reach, s)
-        blocks.append([attended] + exchange(attended))
-    for s in range(seqs):
-        result = finish(section_bits, blocks[s], tokens, s, out_weight, result)
+    last = None
+    for t in range(seqs + 3 * ahead):
+        if t < seqs:
+            after = partners[t - ahead] if t >= ahead else list(notes.values())
+            staged[t] = stage(tokens, t, after)
+            partners[t] = exchange(staged[t])
+            last = staged[t]
+        s = t - 2 * ahead
+        if 0 <= s < seqs:
+            q, kv, rim = pending.pop(s)
+            arrived = partners[t - ahead] if t - ahead < seqs else blocks[s - ahead]
+            last = attend(q, kv, rim, reach, s, arrived)
+            blocks[s] = [last] + exchange(last)
+        s = t - ahead
+        if 0 <= s < seqs:
+            q, kv, tail = project(
+                section_bits, tokens, s, partners[s], scale, gains, qkv_weight, [last]
+            )
+            pending[s] = (q, kv, passed_along(tail, "ctx", 1))
+        s = t - 3 * ahead
+        if 0 <= s < seqs:
+            result = finish(
+                section_bits, blocks[s], tokens, s, out_weight, result, [last]
+            )
     return result
 
 

time: 428 us -> 390 us (0.911)
  blocking collectives: 68.1 us -> 0 us
  waiting for transfers between devices: 194 us -> 224 us
    psum x1 -> x0, blocking collectives: 68.1 us -> none  [per_device(): row_squares = lax.psum(jnp.sum(x_full * x_full, axis=-1), 'feat')]
    ppermute x18 -> x16, waiting for transfers between devices: 194 us -> 219 us  [swapped(): return lax.ppermute(value, axis, pairs)]
    ppermute x0 -> x3, waiting for transfers between devices: none -> 5.27 us  [per_device(): notes[mask] = lax.ppermute(note, 'feat', pairs)]
    ppermute x0 -> x3, starting transfers between devices: none -> 4.39 us  [per_device(): notes[mask] = lax.ppermute(note, 'feat', pairs)]
    unnamed x36 -> x26, local copies, waits for them, and re-layouts: 11 us -> 7.39 us
    ppermute x18 -> x16, starting transfers between devices: 18 us -> 16.6 us  [swapped(): return lax.ppermute(value, axis, pairs)]
  transfers between devices with their start and end apart: 22 -> 23, of which waited for: 9 -> 15; matrix products, arithmetic and copies ran while one was open for 0% -> 0% of each run, Pallas kernels for 27% -> 29%
where the time goes in v2:
time: 390 us; the launch traced here: 387 us
  waiting for transfers between devices  224 us (57%)
  Pallas kernels  122 us (31%)
  starting transfers between devices  28.8 us (7%)
  local copies, waits for them, and re-layouts  8.56 us (2%)
    ppermute x16, waiting for transfers between devices, swapped(): return lax.ppermute(value, axis, pairs)  219 us
    pallas_call x4, Pallas kernels, project(): pl.pallas_call(functools.partial(qkv_kernel, parts, local_blocks, section...  58.5 us
    pallas_call x4, Pallas kernels, finish(): pl.pallas_call(functools.partial(out_kernel, parts, local_blocks, section...  35.4 us
    pallas_call x4, Pallas kernels, attend(): pl.pallas_call(attend_kernel, grid=(width // step,), in_specs=[pl.BlockSp...  22.7 us
    ppermute x16, starting transfers between devices, swapped(): return lax.ppermute(value, axis, pairs)  16.6 us
    ppermute x4, starting transfers between devices, passed_along(): return lax.ppermute(shard, axis, pairs)  7.81 us
  transfers between devices with their start and end apart: 23, of which 15 were waited for; matrix products, arithmetic and copies ran while one was open for 0% of the time, Pallas kernels for 29%

profile of v2, /device:TPU:2, one launch (start us, length us, event | category | flops | bytes accessed | tf_op | source)
XLA Modules:
  0.0 387.2 jit_solution(1068920483498484555)
XLA Ops:
  0.0 3.1 multiply_reduce_fusion
  3.1 0.0 copy-start.9
  3.1 0.7 constant_dynamic-update-slice_fusion
  3.8 1.6 collective-permute-start
  5.4 2.6 collective-permute-start.1
  8.0 0.2 collective-permute-start.2
  8.2 1.9 collective-permute-done.1.rest_1_
  10.1 3.3 collective-permute-done.2.rest_2_
  13.5 2.2 copy-done
  15.7 1.0 stage.6
  16.7 0.8 collective-permute-start.14
  17.5 1.0 stage.4
  18.5 1.2 collective-permute-start.3
  19.8 2.9 collective-permute-start.4
  22.7 0.2 copy.12.refs_3_
  23.0 58.5 %collective-permute-done.13.rest_0_.refs_1_ = bf16[256,2048]{1,0:T(8,128)(2,1)} collective-permute-done((bf16[256,2048]{1,0:T(8,128)(2,1)}, bf16[256,2048]{1,0:T(8,128)(2,1)}, u32[]{:S(2)}, u32[]{:S(2)}) %collective-permute-start.13) | collective-permute-done | bytes 1048608 | tf_op jit(solution)/shard_map/ppermute | solution.py:19
  81.6 2.3 stage.7.refs_6_
  83.8 15.0 %project.6 = (bf16[256,2048]{1,0:T(8,128)(2,1)S(1)}, bf16[2,256,2048]{2,1,0:T(8,128)(2,1)}, bf16[2,128,2048]{2,1,0:T(8,128)(2,1)}) custom-call(s32[5]{0:T(128)S(1)} %copy-done.9, bf16[4,256,2048]{2,1,0:T(8,128)(2,1)} %refs_3_.7, bf16[256,2048]{1,0:T(8,128)(2,1)} %collective-permute-done.13.rest_0_.refs_1_, ...), custom_call_target="tpu_custom_call" | custom-call | flops 4831838208 | bytes 26214400 | tf_op jit(solution)/shard_map/project/pallas_call | solution.py:103
  98.8 1.0 copy-done.5
  99.9 1.9 collective-permute-start.17
  101.8 0.1 collective-permute-start.15
  101.8 3.8 collective-permute-start.16
  105.7 0.2 copy.11.reach_ref
  105.9 3.2 collective-permute-done.4.rest_1_.refs_2_
  109.1 1.3 stage.5.refs_6_
  110.4 14.3 %project.4 = (bf16[256,2048]{1,0:T(8,128)(2,1)S(1)}, bf16[2,256,2048]{2,1,0:T(8,128)(2,1)}, bf16[2,128,2048]{2,1,0:T(8,128)(2,1)}) custom-call(s32[5]{0:T(128)S(1)} %copy-done.9, bf16[4,256,2048]{2,1,0:T(8,128)(2,1)} %refs_3_.7, bf16[256,2048]{1,0:T(8,128)(2,1)S(1)} %collective-permute-done.3.rest_0_.refs_1_, ...), custom_call_target="tpu_custom_call" | custom-call | flops 4831838208 | bytes 26214400 | tf_op jit(solution)/shard_map/project/pallas_call | solution.py:103
  124.7 1.9 collective-permute-start.7
  126.6 0.1 collective-permute-start.5
  126.7 1.1 collective-permute-start.6
  127.8 22.7 %collective-permute-done.15.rest_0_.refs_1_ = bf16[256,2048]{1,0:T(8,128)(2,1)} collective-permute-done((bf16[256,2048]{1,0:T(8,128)(2,1)}, bf16[256,2048]{1,0:T(8,128)(2,1)}, u32[]{:S(2)}, u32[]{:S(2)}) %collective-permute-start.15) | collective-permute-done | bytes 1048608 | tf_op jit(solution)/shard_map/ppermute | solution.py:19
  150.5 3.7 collective-permute-done.16.rest_1_.refs_2_
  154.2 5.7 %attend.6.refs_6_.rest_0_.refs_0_ = bf16[256,2048]{1,0:T(8,128)(2,1)S(1)} custom-call(bf16[256,2048]{1,0:T(8,128)(2,1)S(1)} %copy-done.6, bf16[2,256,2048]{2,1,0:T(8,128)(2,1)} %get-tuple-element.24.kv_ref, bf16[2,128,2048]{2,1,0:T(8,128)(2,1)} %collective-permute-done.17.rim_ref, s32[4,256,1]{2,1,0:T(8,128)S(1)} %copy.11.reach_ref, ...), custom_call_target="tpu_custom_call" | custom-call | flops 536870912 | bytes 5242880 | tf_op jit(solution)/shard_map/attend/pallas_call | solution.py:174
  159.9 15.0 %project.7 = (bf16[256,2048]{1,0:T(8,128)(2,1)S(1)}, bf16[2,256,2048]{2,1,0:T(8,128)(2,1)}, bf16[2,128,2048]{2,1,0:T(8,128)(2,1)}) custom-call(s32[5]{0:T(128)S(1)} %copy-done.9, bf16[4,256,2048]{2,1,0:T(8,128)(2,1)} %refs_3_.7, bf16[256,2048]{1,0:T(8,128)(2,1)} %collective-permute-done.15.rest_0_.refs_1_, ...), custom_call_target="tpu_custom_call" | custom-call | flops 4831838208 | bytes 26214400 | tf_op jit(solution)/shard_map/project/pallas_call | solution.py:103
  174.9 1.9 collective-permute-start.18
  176.8 0.1 collective-permute-start.19
  176.9 1.0 copy-done.7
  177.9 1.9 collective-permute-start.20
  179.8 15.5 %collective-permute-done.5.rest_0_.refs_1_ = bf16[256,2048]{1,0:T(8,128)(2,1)S(1)} collective-permute-done((bf16[256,2048]{1,0:T(8,128)(2,1)S(1)}, bf16[256,2048]{1,0:T(8,128)(2,1)S(1)}, u32[]{:S(2)}, u32[]{:S(2)}) %collective-permute-start.5) | collective-permute-done | bytes 1048608 | tf_op jit(solution)/shard_map/ppermute | solution.py:19
  195.3 3.7 collective-permute-done.6.rest_1_.refs_2_
  199.0 1.2 copy-done.8
  200.3 5.7 %attend.4.refs_6_.rest_0_.refs_0_ = bf16[256,2048]{1,0:T(8,128)(2,1)S(1)} custom-call(bf16[256,2048]{1,0:T(8,128)(2,1)S(1)} %get-tuple-element.17.q_ref, bf16[2,256,2048]{2,1,0:T(8,128)(2,1)} %get-tuple-element.18.kv_ref, bf16[2,128,2048]{2,1,0:T(8,128)(2,1)S(1)} %copy-done.8, s32[4,256,1]{2,1,0:T(8,128)S(1)} %copy.11.reach_ref, ...), custom_call_target="tpu_custom_call" | custom-call | flops 536870912 | bytes 5242880 | tf_op jit(solution)/shard_map/attend/pallas_call | solution.py:174
  205.9 1.1 collective-permute-start.10
  207.1 14.1 %project.5 = (bf16[256,2048]{1,0:T(8,128)(2,1)S(1)}, bf16[2,256,2048]{2,1,0:T(8,128)(2,1)}, bf16[2,128,2048]{2,1,0:T(8,128)(2,1)S(1)}) custom-call(s32[5]{0:T(128)S(1)} %copy-done.9, bf16[4,256,2048]{2,1,0:T(8,128)(2,1)} %refs_3_.7, bf16[256,2048]{1,0:T(8,128)(2,1)S(1)} %collective-permute-done.5.rest_0_.refs_1_, ...), custom_call_target="tpu_custom_call" | custom-call | flops 4831838208 | bytes 26214400 | tf_op jit(solution)/shard_map/project/pallas_call | solution.py:103
  221.2 2.1 collective-permute-start.8
  223.3 0.8 collective-permute-start.9
  224.1 16.2 %collective-permute-done.19.rest_1_.refs_1_ = bf16[256,2048]{1,0:T(8,128)(2,1)S(1)} collective-permute-done((bf16[256,2048]{1,0:T(8,128)(2,1)S(1)}, bf16[256,2048]{1,0:T(8,128)(2,1)S(1)}, u32[]{:S(2)}, u32[]{:S(2)}) %collective-permute-start.19) | collective-permute-done | bytes 1048608 | tf_op jit(solution)/shard_map/ppermute | solution.py:19
  240.3 26.1 %collective-permute-done.20.rest_2_.refs_2_ = bf16[256,2048]{1,0:T(8,128)(2,1)S(1)} collective-permute-done((bf16[256,2048]{1,0:T(8,128)(2,1)S(1)}, bf16[256,2048]{1,0:T(8,128)(2,1)S(1)}, u32[]{:S(2)}, u32[]{:S(2)}) %collective-permute-start.20) | collective-permute-done | bytes 1048608 | tf_op jit(solution)/shard_map/ppermute | solution.py:19
  266.4 1.0 copy-done.1
  267.4 5.7 %attend.7.refs_5_.refs_0_ = bf16[256,2048]{1,0:T(8,128)(2,1)S(1)} custom-call(bf16[256,2048]{1,0:T(8,128)(2,1)S(1)} %get-tuple-element.26.q_ref, bf16[2,256,2048]{2,1,0:T(8,128)(2,1)} %get-tuple-element.27.kv_ref, bf16[2,128,2048]{2,1,0:T(8,128)(2,1)S(1)} %collective-permute-done.18.rim_ref, s32[4,256,1]{2,1,0:T(8,128)S(1)} %copy.11.reach_ref, ...), custom_call_target="tpu_custom_call" | custom-call | flops 536870912 | bytes 5242880 | tf_op jit(solution)/shard_map/attend/pallas_call | solution.py:174
  273.1 0.1 collective-permute-start.21
  273.1 0.8 collective-permute-start.22
  274.0 15.0 %collective-permute-done.10.rest_2_.refs_2_ = bf16[256,2048]{1,0:T(8,128)(2,1)S(1)} collective-permute-done((bf16[256,2048]{1,0:T(8,128)(2,1)S(1)}, bf16[256,2048]{1,0:T(8,128)(2,1)S(1)}, u32[]{:S(2)}, u32[]{:S(2)}) %collective-permute-start.10) | collective-permute-done | bytes 1048608 | tf_op jit(solution)/shard_map/ppermute | solution.py:19
  289.0 1.0 copy-done.3
  289.9 5.7 %attend.5.refs_6_.refs_0_ = bf16[256,2048]{1,0:T(8,128)(2,1)S(1)} custom-call(bf16[256,2048]{1,0:T(8,128)(2,1)S(1)} %get-tuple-element.20.q_ref, bf16[2,256,2048]{2,1,0:T(8,128)(2,1)} %get-tuple-element.21.kv_ref, bf16[2,128,2048]{2,1,0:T(8,128)(2,1)S(1)} %collective-permute-done.8.rim_ref, s32[4,256,1]{2,1,0:T(8,128)S(1)} %copy.11.reach_ref, ...), custom_call_target="tpu_custom_call" | custom-call | flops 536870912 | bytes 5242880 | tf_op jit(solution)/shard_map/attend/pallas_call | solution.py:174
  295.6 0.1 collective-permute-start.11
  295.7 1.7 collective-permute-start.12
  297.4 8.8 %finish.4.refs_5_ = f32[4,256,2048]{2,1,0:T(8,128)} custom-call(s32[5]{0:T(128)S(1)} %copy-done.9, bf16[256,2048]{1,0:T(8,128)(2,1)S(1)} %attend.6.refs_6_.rest_0_.refs_0_, bf16[256,2048]{1,0:T(8,128)(2,1)S(1)} %collective-permute-done.19.rest_1_.refs_1_, bf16[256,2048]{1,0:T(8,128)(2,1)S(1)} %copy-done.2, bf16[4,256,2048]{2,1,0:T(8,128)(2,1)} %refs_3_.7, ...), custom_call_target="tpu_custom_call" | custom-call | flops 1610612736 | bytes 12582912 | tf_op jit(solution)/shard_map/finish/pallas_call | solution.py:223
  306.3 8.8 %finish.5.refs_5_ = f32[4,256,2048]{2,1,0:T(8,128)} custom-call(s32[5]{0:T(128)S(1)} %copy-done.9, bf16[256,2048]{1,0:T(8,128)(2,1)S(1)} %attend.4.refs_6_.rest_0_.refs_0_, bf16[256,2048]{1,0:T(8,128)(2,1)S(1)} %collective-permute-done.9.rest_1_.refs_1_, bf16[256,2048]{1,0:T(8,128)(2,1)S(1)} %copy-done.4, ...), custom_call_target="tpu_custom_call", output_to_operand_aliasing={{}: (6, {})} | custom-call | flops 1610612736 | bytes 12582912 | tf_op jit(solution)/shard_map/finish/pallas_call | solution.py:223
  315.1 17.6 %collective-permute-done.21.refs_1_ = bf16[256,2048]{1,0:T(8,128)(2,1)S(1)} collective-permute-done((bf16[256,2048]{1,0:T(8,128)(2,1)S(1)}, bf16[256,2048]{1,0:T(8,128)(2,1)S(1)}, u32[]{:S(2)}, u32[]{:S(2)}) %collective-permute-start.21) | collective-permute-done | bytes 1048608 | tf_op jit(solution)/shard_map/ppermute | solution.py:19
  332.7 1.3 collective-permute-done.22.refs_2_
  333.9 8.8 %finish.6.refs_5_ = f32[4,256,2048]{2,1,0:T(8,128)} custom-call(s32[5]{0:T(128)S(1)} %copy-done.9, bf16[256,2048]{1,0:T(8,128)(2,1)S(1)} %attend.7.refs_5_.refs_0_, bf16[256,2048]{1,0:T(8,128)(2,1)S(1)} %collective-permute-done.21.refs_1_, bf16[256,2048]{1,0:T(8,128)(2,1)S(1)} %collective-permute-done.22.refs_2_, ...), custom_call_target="tpu_custom_call", output_to_operand_aliasing={{}: (6, {})} | custom-call | flops 1610612736 | bytes 12582912 | tf_op jit(solution)/shard_map/finish/pallas_call | solution.py:223
  342.8 33.9 %collective-permute-done.11.refs_1_ = bf16[256,2048]{1,0:T(8,128)(2,1)S(1)} collective-permute-done((bf16[256,2048]{1,0:T(8,128)(2,1)S(1)}, bf16[256,2048]{1,0:T(8,128)(2,1)S(1)}, u32[]{:S(2)}, u32[]{:S(2)}) %collective-permute-start.11) | collective-permute-done | bytes 1048608 | tf_op jit(solution)/shard_map/ppermute | solution.py:19
  376.7 1.7 collective-permute-done.12.refs_2_
  378.4 8.8 %finish.7 = f32[4,256,2048]{2,1,0:T(8,128)} custom-call(s32[5]{0:T(128)S(1)} %copy-done.9, bf16[256,2048]{1,0:T(8,128)(2,1)S(1)} %attend.5.refs_6_.refs_0_, bf16[256,2048]{1,0:T(8,128)(2,1)S(1)} %collective-permute-done.11.refs_1_, bf16[256,2048]{1,0:T(8,128)(2,1)S(1)} %collective-permute-done.12.refs_2_, ...), custom_call_target="tpu_custom_call", output_to_operand_aliasing={{}: (6, {})} | custom-call | flops 1610612736 | bytes 12582912 | tf_op jit(solution)/shard_map/finish/pallas_call | solution.py:223
  (36 shorter events, 0.1 us)
Async XLA Ops:
  0.0 23.0 %copy-start.10 = (f32[2048]{0:T(1024)S(1)}, f32[2048]{0:T(1024)}, u32[]{:S(2)}) copy-start(f32[2048]{0:T(1024)} %param.7) | copy-start | bytes 24580
  3.1 80.7 %copy-start.9 = (s32[5]{0:T(128)S(1)}, s32[5]{0:T(128)}, u32[]{:S(2)}) copy-start(s32[5]{0:T(128)} %bits_ref.15) | copy-start | bytes 64
  3.8 4.4 %collective-permute-start = (f32[3072]{0:T(1024)S(1)}, f32[3072]{0:T(1024)S(1)}, u32[]{:S(2)}, u32[]{:S(2)}) collective-permute-start(f32[3072]{0:T(1024)S(1)} %constant_dynamic-update-slice_fusion), channel_id=1, source_target_pairs={{0,1},{1,0},{2,3},{3,2},{4,5},{5,4},{6,7},{7,6},{8,9},{9,8},{10,11... | collective-permute-start | bytes 36872 | tf_op jit(solution)/shard_map/ppermute | solution.py:269
  5.4 4.7 %collective-permute-start.1 = (f32[3072]{0:T(1024)S(1)}, f32[3072]{0:T(1024)S(1)}, u32[]{:S(2)}, u32[]{:S(2)}) collective-permute-start(f32[3072]{0:T(1024)S(1)} %constant_dynamic-update-slice_fusion), channel_id=1, source_target_pairs={{0,2},{1,3},{2,0},{3,1},{4,6},{5,7},{6,4},{7,5},{8,10},{9,11},{10,... | collective-permute-start | bytes 36872 | tf_op jit(solution)/shard_map/ppermute | solution.py:269
  8.0 5.5 %collective-permute-start.2 = (f32[3072]{0:T(1024)S(1)}, f32[3072]{0:T(1024)S(1)}, u32[]{:S(2)}, u32[]{:S(2)}) collective-permute-start(f32[3072]{0:T(1024)S(1)} %constant_dynamic-update-slice_fusion), channel_id=1, source_target_pairs={{0,3},{1,2},{2,1},{3,0},{4,7},{5,6},{6,5},{7,4},{8,11},{9,10},{10,... | collective-permute-start | bytes 36872 | tf_op jit(solution)/shard_map/ppermute | solution.py:269
  13.5 2.2 copy-start
  16.7 64.8 %collective-permute-start.13 = (bf16[256,2048]{1,0:T(8,128)(2,1)}, bf16[256,2048]{1,0:T(8,128)(2,1)}, u32[]{:S(2)}, u32[]{:S(2)}) collective-permute-start(bf16[256,2048]{1,0:T(8,128)(2,1)} %stage.6), channel_id=1, source_target_pairs={{0,1},{1,0},{2,3},{3,2},{4,5},{5,4},{6,7},{7,6},{8,9},{9,8},{10,11... | collective-permute-start | bytes 3145736 | tf_op jit(solution)/shard_map/ppermute | solution.py:19
  16.7 64.8 %collective-permute-start.14 = (bf16[256,2048]{1,0:T(8,128)(2,1)}, bf16[256,2048]{1,0:T(8,128)(2,1)}, u32[]{:S(2)}, u32[]{:S(2)}) collective-permute-start(bf16[256,2048]{1,0:T(8,128)(2,1)} %stage.6), channel_id=1, source_target_pairs={{0,2},{1,3},{2,0},{3,1},{4,6},{5,7},{6,4},{7,5},{8,10},{9,11},{10,... | collective-permute-start | bytes 3145736 | tf_op jit(solution)/shard_map/ppermute | solution.py:19
  18.5 87.4 %collective-permute-start.3 = (bf16[256,2048]{1,0:T(8,128)(2,1)}, bf16[256,2048]{1,0:T(8,128)(2,1)S(1)}, u32[]{:S(2)}, u32[]{:S(2)}) collective-permute-start(bf16[256,2048]{1,0:T(8,128)(2,1)} %stage.4), channel_id=1, source_target_pairs={{0,1},{1,0},{2,3},{3,2},{4,5},{5,4},{6,7},{7,6},{8,9},{9,8},{10,11... | collective-permute-start | bytes 3145736 | tf_op jit(solution)/shard_map/ppermute | solution.py:19
  19.8 89.3 %collective-permute-start.4 = (bf16[256,2048]{1,0:T(8,128)(2,1)}, bf16[256,2048]{1,0:T(8,128)(2,1)S(1)}, u32[]{:S(2)}, u32[]{:S(2)}) collective-permute-start(bf16[256,2048]{1,0:T(8,128)(2,1)} %stage.4), channel_id=1, source_target_pairs={{0,2},{1,3},{2,0},{3,1},{4,6},{5,7},{6,4},{7,5},{8,10},{9,11},{10,... | collective-permute-start | bytes 3145736 | tf_op jit(solution)/shard_map/ppermute | solution.py:19
  83.8 21.8 %copy-start.11 = (s32[4,256]{1,0:T(4,128)S(1)}, s32[4,256]{1,0:T(4,128)}, u32[]{:S(2)}) copy-start(s32[4,256]{1,0:T(4,128)} %param.11) | copy-start | bytes 12292
  98.8 1.0 copy-start.5
  99.9 26.8 %collective-permute-start.17 = (bf16[2,128,2048]{2,1,0:T(8,128)(2,1)}, bf16[2,128,2048]{2,1,0:T(8,128)(2,1)}, u32[]{:S(2)}, u32[]{:S(2)}) collective-permute-start(bf16[2,128,2048]{2,1,0:T(8,128)(2,1)} %get-tuple-element.25), channel_id=1, source_target_pairs={{0,4},{4,8},{8,12},{12,16},{16,20},{20,24},{24,28},{1,5},{5,9},{9,... | collective-permute-start | bytes 3145736 | tf_op jit(solution)/shard_map/ppermute | solution.py:25
  101.8 48.7 %collective-permute-start.15 = (bf16[256,2048]{1,0:T(8,128)(2,1)}, bf16[256,2048]{1,0:T(8,128)(2,1)}, u32[]{:S(2)}, u32[]{:S(2)}) collective-permute-start(bf16[256,2048]{1,0:T(8,128)(2,1)} %stage.7.refs_6_), channel_id=1, source_target_pairs={{0,1},{1,0},{2,3},{3,2},{4,5},{5,4},{6,7},{7,6},{8,9},{9,8},{10,11... | collective-permute-start | bytes 3145736 | tf_op jit(solution)/shard_map/ppermute | solution.py:19
  101.8 52.3 %collective-permute-start.16 = (bf16[256,2048]{1,0:T(8,128)(2,1)}, bf16[256,2048]{1,0:T(8,128)(2,1)}, u32[]{:S(2)}, u32[]{:S(2)}) collective-permute-start(bf16[256,2048]{1,0:T(8,128)(2,1)} %stage.7.refs_6_), channel_id=1, source_target_pairs={{0,2},{1,3},{2,0},{3,1},{4,6},{5,7},{6,4},{7,5},{8,10},{9,11},{10,... | collective-permute-start | bytes 3145736 | tf_op jit(solution)/shard_map/ppermute | solution.py:19
  110.4 43.8 %copy-start.6 = (bf16[256,2048]{1,0:T(8,128)(2,1)S(1)}, bf16[256,2048]{1,0:T(8,128)(2,1)}, u32[]{:S(2)}) copy-start(bf16[256,2048]{1,0:T(8,128)(2,1)} %copy-done.5) | copy-start | bytes 3145732
  124.7 52.2 %collective-permute-start.7 = (bf16[2,128,2048]{2,1,0:T(8,128)(2,1)}, bf16[2,128,2048]{2,1,0:T(8,128)(2,1)S(1)}, u32[]{:S(2)}, u32[]{:S(2)}) collective-permute-start(bf16[2,128,2048]{2,1,0:T(8,128)(2,1)} %get-tuple-element.19), channel_id=1, source_target_pairs={{0,4},{4,8},{8,12},{12,16},{16,20},{20,24},{24,28},{1,5},{5,9},{9,... | collective-permute-start | bytes 3145736 | tf_op jit(solution)/shard_map/ppermute | solution.py:25
  126.6 68.7 %collective-permute-start.5 = (bf16[256,2048]{1,0:T(8,128)(2,1)S(1)}, bf16[256,2048]{1,0:T(8,128)(2,1)S(1)}, u32[]{:S(2)}, u32[]{:S(2)}) collective-permute-start(bf16[256,2048]{1,0:T(8,128)(2,1)S(1)} %stage.5.refs_6_), channel_id=1, source_target_pairs={{0,1},{1,0},{2,3},{3,2},{4,5},{5,4},{6,7},{7,6},{8,9},{9,8},{10,11... | collective-permute-start | bytes 3145736 | tf_op jit(solution)/shard_map/ppermute | solution.py:19
  126.7 72.3 %collective-permute-start.6 = (bf16[256,2048]{1,0:T(8,128)(2,1)S(1)}, bf16[256,2048]{1,0:T(8,128)(2,1)S(1)}, u32[]{:S(2)}, u32[]{:S(2)}) collective-permute-start(bf16[256,2048]{1,0:T(8,128)(2,1)S(1)} %stage.5.refs_6_), channel_id=1, source_target_pairs={{0,2},{1,3},{2,0},{3,1},{4,6},{5,7},{6,4},{7,5},{8,10},{9,11},{10,... | collective-permute-start | bytes 3145736 | tf_op jit(solution)/shard_map/ppermute | solution.py:19
  174.9 48.4 %collective-permute-start.18 = (bf16[2,128,2048]{2,1,0:T(8,128)(2,1)}, bf16[2,128,2048]{2,1,0:T(8,128)(2,1)S(1)}, u32[]{:S(2)}, u32[]{:S(2)}) collective-permute-start(bf16[2,128,2048]{2,1,0:T(8,128)(2,1)} %get-tuple-element.28), channel_id=1, source_target_pairs={{0,4},{4,8},{8,12},{12,16},{16,20},{20,24},{24,28},{1,5},{5,9},{9,... | collective-permute-start | bytes 3145736 | tf_op jit(solution)/shard_map/ppermute | solution.py:25
  176.8 63.5 %collective-permute-start.19 = (bf16[256,2048]{1,0:T(8,128)(2,1)S(1)}, bf16[256,2048]{1,0:T(8,128)(2,1)S(1)}, u32[]{:S(2)}, u32[]{:S(2)}) collective-permute-start(bf16[256,2048]{1,0:T(8,128)(2,1)S(1)} %attend.6.refs_6_.rest_0_.refs_0_), channel_id=1, source_target_pairs={{0,1},{1,0},{2,3},{3,2},{4,5},{5,4},{6,7},{7,6},{8,9},{9,8},{10,11... | collective-permute-start | bytes 3145736 | tf_op jit(solution)/shard_map/ppermute | solution.py:19
  176.9 1.0 copy-start.7
  177.9 88.5 %collective-permute-start.20 = (bf16[256,2048]{1,0:T(8,128)(2,1)S(1)}, bf16[256,2048]{1,0:T(8,128)(2,1)S(1)}, u32[]{:S(2)}, u32[]{:S(2)}) collective-permute-start(bf16[256,2048]{1,0:T(8,128)(2,1)S(1)} %attend.6.refs_6_.rest_0_.refs_0_), channel_id=1, source_target_pairs={{0,2},{1,3},{2,0},{3,1},{4,6},{5,7},{6,4},{7,5},{8,10},{9,11},{10,... | collective-permute-start | bytes 3145736 | tf_op jit(solution)/shard_map/ppermute | solution.py:19
  199.0 1.2 copy-start.8
  205.9 83.0 %collective-permute-start.10 = (bf16[256,2048]{1,0:T(8,128)(2,1)S(1)}, bf16[256,2048]{1,0:T(8,128)(2,1)S(1)}, u32[]{:S(2)}, u32[]{:S(2)}) collective-permute-start(bf16[256,2048]{1,0:T(8,128)(2,1)S(1)} %attend.4.refs_6_.rest_0_.refs_0_), channel_id=1, source_target_pairs={{0,2},{1,3},{2,0},{3,1},{4,6},{5,7},{6,4},{7,5},{8,10},{9,11},{10,... | collective-permute-start | bytes 3145736 | tf_op jit(solution)/shard_map/ppermute | solution.py:19
  221.2 52.7 %collective-permute-start.8 = (bf16[2,128,2048]{2,1,0:T(8,128)(2,1)S(1)}, bf16[2,128,2048]{2,1,0:T(8,128)(2,1)S(1)}, u32[]{:S(2)}, u32[]{:S(2)}) collective-permute-start(bf16[2,128,2048]{2,1,0:T(8,128)(2,1)S(1)} %get-tuple-element.22), channel_id=1, source_target_pairs={{0,4},{4,8},{8,12},{12,16},{16,20},{20,24},{24,28},{1,5},{5,9},{9,... | collective-permute-start | bytes 3145736 | tf_op jit(solution)/shard_map/ppermute | solution.py:25
  223.3 65.7 %collective-permute-start.9 = (bf16[256,2048]{1,0:T(8,128)(2,1)S(1)}, bf16[256,2048]{1,0:T(8,128)(2,1)S(1)}, u32[]{:S(2)}, u32[]{:S(2)}) collective-permute-start(bf16[256,2048]{1,0:T(8,128)(2,1)S(1)} %attend.4.refs_6_.rest_0_.refs_0_), channel_id=1, source_target_pairs={{0,1},{1,0},{2,3},{3,2},{4,5},{5,4},{6,7},{7,6},{8,9},{9,8},{10,11... | collective-permute-start | bytes 3145736 | tf_op jit(solution)/shard_map/ppermute | solution.py:19
  266.4 1.0 copy-start.1
  273.1 24.3 %copy-start.2 = (bf16[256,2048]{1,0:T(8,128)(2,1)S(1)}, bf16[256,2048]{1,0:T(8,128)(2,1)}, u32[]{:S(2)}) copy-start(bf16[256,2048]{1,0:T(8,128)(2,1)} %copy-done.1) | copy-start | bytes 3145732
  273.1 59.6 %collective-permute-start.21 = (bf16[256,2048]{1,0:T(8,128)(2,1)S(1)}, bf16[256,2048]{1,0:T(8,128)(2,1)S(1)}, u32[]{:S(2)}, u32[]{:S(2)}) collective-permute-start(bf16[256,2048]{1,0:T(8,128)(2,1)S(1)} %attend.7.refs_5_.refs_0_), channel_id=1, source_target_pairs={{0,1},{1,0},{2,3},{3,2},{4,5},{5,4},{6,7},{7,6},{8,9},{9,8},{10,11... | collective-permute-start | bytes 3145736 | tf_op jit(solution)/shard_map/ppermute | solution.py:19
  273.1 60.8 %collective-permute-start.22 = (bf16[256,2048]{1,0:T(8,128)(2,1)S(1)}, bf16[256,2048]{1,0:T(8,128)(2,1)S(1)}, u32[]{:S(2)}, u32[]{:S(2)}) collective-permute-start(bf16[256,2048]{1,0:T(8,128)(2,1)S(1)} %attend.7.refs_5_.refs_0_), channel_id=1, source_target_pairs={{0,2},{1,3},{2,0},{3,1},{4,6},{5,7},{6,4},{7,5},{8,10},{9,11},{10,... | collective-permute-start | bytes 3145736 | tf_op jit(solution)/shard_map/ppermute | solution.py:19
  289.0 1.0 copy-start.3
  295.6 81.1 %collective-permute-start.11 = (bf16[256,2048]{1,0:T(8,128)(2,1)S(1)}, bf16[256,2048]{1,0:T(8,128)(2,1)S(1)}, u32[]{:S(2)}, u32[]{:S(2)}) collective-permute-start(bf16[256,2048]{1,0:T(8,128)(2,1)S(1)} %attend.5.refs_6_.refs_0_), channel_id=1, source_target_pairs={{0,1},{1,0},{2,3},{3,2},{4,5},{5,4},{6,7},{7,6},{8,9},{9,8},{10,11... | collective-permute-start | bytes 3145736 | tf_op jit(solution)/shard_map/ppermute | solution.py:19
  295.7 82.7 %collective-permute-start.12 = (bf16[256,2048]{1,0:T(8,128)(2,1)S(1)}, bf16[256,2048]{1,0:T(8,128)(2,1)S(1)}, u32[]{:S(2)}, u32[]{:S(2)}) collective-permute-start(bf16[256,2048]{1,0:T(8,128)(2,1)S(1)} %attend.5.refs_6_.refs_0_), channel_id=1, source_target_pairs={{0,2},{1,3},{2,0},{3,1},{4,6},{5,7},{6,4},{7,5},{8,10},{9,11},{10,... | collective-permute-start | bytes 3145736 | tf_op jit(solution)/shard_map/ppermute | solution.py:19
  297.4 8.9 %copy-start.4 = (bf16[256,2048]{1,0:T(8,128)(2,1)S(1)}, bf16[256,2048]{1,0:T(8,128)(2,1)}, u32[]{:S(2)}) copy-start(bf16[256,2048]{1,0:T(8,128)(2,1)} %copy-done.3) | copy-start | bytes 3145732

commit v3 on v2

--- a/solution.py
+++ b/solution.py
@@ -248,6 +248,103 @@
     )(section_bits, *blocks, tokens, weight, *earlier)
 
 
+def near_kernel(local_blocks, own_sections, sec_ref, *refs):
+    a_ref, x_ref, w_ref = refs[:3]
+    out_ref, gathered = refs[-2:]
+    i = pl.program_id(0)
+    block = w_ref.shape[-1]
+
+    @pl.when(i == 0)
+    def _():
+        for b in range(local_blocks):
+            gathered[b] = a_ref[:, b * block : (b + 1) * block]
+
+    out = x_ref[0].astype(jnp.float32)
+    out = out + jnp.dot(
+        gathered[i], w_ref[0, :block], preferred_element_type=jnp.float32
+    )
+    for bit in range(own_sections):
+        first = pl.multiple_of(sec_ref[bit] * block, block)
+        out = out + jnp.dot(
+            gathered[lax.bitwise_xor(i, jnp.int32(1 << bit))],
+            w_ref[0, pl.ds(first, block)],
+            preferred_element_type=jnp.float32,
+        )
+    out_ref[0] = out
+
+
+def finish_near(sections_of, attended, tokens, s, weight, result, after):
+    seqs, rows, width = tokens.shape
+    local_blocks, depth, block = weight.shape
+    one = lambda i, sec: (s, 0, i)
+    earlier = ([] if result is None else [result]) + after
+    return pl.pallas_call(
+        functools.partial(near_kernel, local_blocks, local_blocks.bit_length() - 1),
+        grid_spec=pltpu.PrefetchScalarGridSpec(
+            num_scalar_prefetch=1,
+            grid=(local_blocks,),
+            in_specs=[
+                pl.BlockSpec((rows, width), lambda i, sec: (0, 0)),
+                pl.BlockSpec((1, rows, block), one),
+                pl.BlockSpec((1, depth, block), lambda i, sec: (i, 0, 0)),
+            ]
+            + [pl.BlockSpec(memory_space=pl.ANY)] * len(earlier),
+            out_specs=pl.BlockSpec((1, rows, block), one),
+            scratch_shapes=[pltpu.VMEM((local_blocks, rows, block), jnp.bfloat16)],
+        ),
+        out_shape=jax.ShapeDtypeStruct(tokens.shape, jnp.float32),
+        input_output_aliases={} if result is None else {4: 0},
+        compiler_params=params(),
+        cost_estimate=pl.CostEstimate(
+            flops=2 * rows * depth * width,
+            bytes_accessed=2 * weight.size + 8 * rows * width,
+            transcendentals=0,
+        ),
+        name="finish_near",
+    )(sections_of, attended, tokens, weight, *earlier)
+
+
+def far_kernel(parts, sec_ref, *refs):
+    out = refs[2 * parts][0]
+    for part in range(parts):
+        out = out + jnp.dot(
+            refs[part][...], refs[parts + part][0], preferred_element_type=jnp.float32
+        )
+    refs[-1][0] = out
+
+
+def finish_far(sections_of, partners, s, weight, result):
+    seqs, rows, width = result.shape
+    local_blocks, depth, block = weight.shape
+    local_bits = local_blocks.bit_length() - 1
+    parts = len(partners)
+    one = pl.BlockSpec((1, rows, block), lambda i, sec: (s, 0, i))
+    weight_of = [
+        pl.BlockSpec((1, block, block), lambda i, sec, at=local_bits + d: (i, sec[at], 0))
+        for d in range(parts)
+    ]
+    return pl.pallas_call(
+        functools.partial(far_kernel, parts),
+        grid_spec=pltpu.PrefetchScalarGridSpec(
+            num_scalar_prefetch=1,
+            grid=(local_blocks,),
+            in_specs=[pl.BlockSpec((rows, block), lambda i, sec: (0, i))] * parts
+            + weight_of
+            + [one],
+            out_specs=one,
+        ),
+        out_shape=jax.ShapeDtypeStruct(result.shape, jnp.float32),
+        input_output_aliases={1 + 2 * parts: 0},
+        compiler_params=params(),
+        cost_estimate=pl.CostEstimate(
+            flops=2 * rows * parts * block * width,
+            bytes_accessed=2 * parts * block * width + rows * width * (2 * parts + 8),
+            transcendentals=0,
+        ),
+        name="finish_far",
+    )(sections_of, *partners, *[weight] * parts, result)
+
+
 def per_device(tokens, norm_gain, qkv_weight, out_weight, section_bits, positions):
     seqs, rows, width = tokens.shape
     _, local_blocks, terms, block, _ = qkv_weight.shape
@@ -275,13 +372,20 @@
     index = lax.axis_index("ctx") * rows + jnp.arange(rows, dtype=jnp.int32)
     reach = jnp.minimum(jnp.minimum(positions, index), WINDOW - 1)[..., None]
 
+    bit_ids = jnp.arange(section_bits.shape[0], dtype=jnp.int32)
+    hits = section_bits[None, :] == bit_ids[:, None]
+    sections_of = 1 + jnp.sum(jnp.where(hits, bit_ids[None, :], 0), axis=1)
+    sections_of = sections_of.astype(jnp.int32)
+
     ahead = 2
     staged, partners, blocks, pending = {}, {}, {}, {}
     result = None
     last = None
     for t in range(seqs + 3 * ahead):
         if t < seqs:
-            after = partners[t - ahead] if t >= ahead else list(notes.values())
+            after = partners[t - ahead] if t >= ahead else [note]
+            if t == 1:
+                after = list(notes.values())
             staged[t] = stage(tokens, t, after)
             partners[t] = exchange(staged[t])
             last = staged[t]
@@ -299,9 +403,15 @@
             pending[s] = (q, kv, passed_along(tail, "ctx", 1))
         s = t - 3 * ahead
         if 0 <= s < seqs:
-            result = finish(
-                section_bits, blocks[s], tokens, s, out_weight, result, [last]
-            )
+            if s < seqs - 1:
+                result = finish(
+                    section_bits, blocks[s], tokens, s, out_weight, result, [last]
+                )
+            else:
+                result = finish_near(
+                    sections_of, blocks[s][0], tokens, s, out_weight, result, [last]
+                )
+                result = finish_far(sections_of, blocks[s][1:], s, out_weight, result)
     return result
 
 

time: 390 us -> 387 us (level)
  waiting for transfers between devices: 224 us -> 204 us
  starting transfers between devices: 28.8 us -> 38.4 us
  Pallas kernels: 122 us -> 129 us
    ppermute x16, waiting for transfers between devices: 219 us -> 162 us  [swapped(): return lax.ppermute(value, axis, pairs)]
    ppermute x3, waiting for transfers between devices: 5.27 us -> 42.2 us  [per_device(): notes[mask] = lax.ppermute(note, 'feat', pairs)]
    pallas_call x0 -> x2, Pallas kernels: none -> 15.7 us  [the longest x1 8.22 us: finish_near(): pl.pallas_call(functools.partial(near_kernel, local_blocks, local_blocks....]
    ppermute x16, starting transfers between devices: 16.6 us -> 26.2 us  [swapped(): return lax.ppermute(value, axis, pairs)]
    pallas_call x4 -> x3, Pallas kernels: 35.4 us -> 26.6 us  [finish(): pl.pallas_call(functools.partial(out_kernel, parts, local_blocks, section...]
  transfers between devices with their start and end apart: 23 -> 23, of which waited for: 15 -> 11; matrix products, arithmetic and copies ran while one was open for 0% -> 0% of each run, Pallas kernels for 29% -> 31%
where the time goes in v3:
time: 387 us; the launch traced here: 384 us
  waiting for transfers between devices  204 us (53%)
  Pallas kernels  129 us (33%)
  starting transfers between devices  38.4 us (10%)
  local copies, waits for them, and re-layouts  8.61 us (2%)
    ppermute x16, waiting for transfers between devices, swapped(): return lax.ppermute(value, axis, pairs)  162 us
    pallas_call x4, Pallas kernels, project(): pl.pallas_call(functools.partial(qkv_kernel, parts, local_blocks, section...  58.7 us
    ppermute x3, waiting for transfers between devices, per_device(): notes[mask] = lax.ppermute(note, 'feat', pairs)  42.2 us
    pallas_call x3, Pallas kernels, finish(): pl.pallas_call(functools.partial(out_kernel, parts, local_blocks, section...  26.6 us
    ppermute x16, starting transfers between devices, swapped(): return lax.ppermute(value, axis, pairs)  26.2 us
    pallas_call x4, Pallas kernels, attend(): pl.pallas_call(attend_kernel, grid=(width // step,), in_specs=[pl.BlockSp...  22.7 us
    pallas_call x1, Pallas kernels, finish_near(): pl.pallas_call(functools.partial(near_kernel, local_blocks, local_blocks....  8.22 us
    ppermute x4, starting transfers between devices, passed_along(): return lax.ppermute(shard, axis, pairs)  7.81 us
  transfers between devices with their start and end apart: 23, of which 11 were waited for; matrix products, arithmetic and copies ran while one was open for 0% of the time, Pallas kernels for 31%

profile of v3, /device:TPU:2, one launch (start us, length us, event | category | flops | bytes accessed | tf_op | source)
XLA Modules:
  0.0 383.7 jit_solution(15270296467058346995)
XLA Ops:
  0.0 3.1 multiply_reduce_fusion
  3.1 0.7 constant_dynamic-update-slice_fusion.rest_0_
  3.8 2.2 copy-done
  6.0 1.1 stage.6
  7.1 1.6 collective-permute-start.13
  8.6 2.6 collective-permute-start.14
  11.2 0.4 collective-permute-start
  11.7 0.3 collective-permute-start.1
  12.0 3.6 collective-permute-start.2
  15.6 39.0 %collective-permute-done.rest_0_ = f32[3072]{0:T(1024)S(1)} collective-permute-done((f32[3072]{0:T(1024)S(1)}, f32[3072]{0:T(1024)S(1)}, u32[]{:S(2)}, u32[]{:S(2)}) %collective-permute-start) | collective-permute-done | bytes 12320 | tf_op jit(solution)/shard_map/ppermute | solution.py:366
  54.6 3.2 collective-permute-done.1.rest_1_
  57.8 1.0 stage.4
  58.9 0.7 collective-permute-start.3
  59.6 2.3 collective-permute-start.4
  61.9 0.2 copy.21.refs_3_
  62.2 0.0 collective-permute-done.13.rest_0_.refs_1_
  62.2 2.3 stage.7.refs_6_
  64.5 15.0 %project.6 = (bf16[256,2048]{1,0:T(8,128)(2,1)S(1)}, bf16[2,256,2048]{2,1,0:T(8,128)(2,1)}, bf16[2,128,2048]{2,1,0:T(8,128)(2,1)}) custom-call(s32[5]{0:T(128)S(1)} %copy-done.10, bf16[4,256,2048]{2,1,0:T(8,128)(2,1)} %refs_1_.1, bf16[256,2048]{1,0:T(8,128)(2,1)} %collective-permute-done.13.rest_0_.refs_1_, ...), custom_call_target="tpu_custom_call" | custom-call | flops 4831838208 | bytes 26214400 | tf_op jit(solution)/shard_map/project/pallas_call | solution.py:103
  79.5 1.0 copy-done.6
  80.6 1.9 collective-permute-start.17
  82.5 0.8 collective-permute-start.15
  83.2 1.2 collective-permute-start.16
  84.5 0.2 copy.20.reach_ref
  84.7 41.5 %collective-permute-done.3.rest_0_.refs_1_ = bf16[256,2048]{1,0:T(8,128)(2,1)S(1)} collective-permute-done((bf16[256,2048]{1,0:T(8,128)(2,1)}, bf16[256,2048]{1,0:T(8,128)(2,1)S(1)}, u32[]{:S(2)}, u32[]{:S(2)}) %collective-permute-start.3) | collective-permute-done | bytes 1048608 | tf_op jit(solution)/shard_map/ppermute | solution.py:19
  126.2 1.3 stage.5.refs_6_
  127.5 14.3 %project.4 = (bf16[256,2048]{1,0:T(8,128)(2,1)S(1)}, bf16[2,256,2048]{2,1,0:T(8,128)(2,1)}, bf16[2,128,2048]{2,1,0:T(8,128)(2,1)}) custom-call(s32[5]{0:T(128)S(1)} %copy-done.10, bf16[4,256,2048]{2,1,0:T(8,128)(2,1)} %refs_1_.1, bf16[256,2048]{1,0:T(8,128)(2,1)S(1)} %collective-permute-done.3.rest_0_.refs_1_, ...), custom_call_target="tpu_custom_call" | custom-call | flops 4831838208 | bytes 26214400 | tf_op jit(solution)/shard_map/project/pallas_call | solution.py:103
  141.8 1.9 collective-permute-start.7
  143.8 0.1 collective-permute-start.5
  143.8 0.0 collective-permute-done.17.rim_ref
  143.8 1.8 collective-permute-start.6
  145.6 8.4 %collective-permute-done.15.rest_0_.refs_1_ = bf16[256,2048]{1,0:T(8,128)(2,1)} collective-permute-done((bf16[256,2048]{1,0:T(8,128)(2,1)}, bf16[256,2048]{1,0:T(8,128)(2,1)}, u32[]{:S(2)}, u32[]{:S(2)}) %collective-permute-start.15) | collective-permute-done | bytes 1048608 | tf_op jit(solution)/shard_map/ppermute | solution.py:19
  154.0 5.7 %attend.6.refs_6_.rest_0_.refs_0_ = bf16[256,2048]{1,0:T(8,128)(2,1)S(1)} custom-call(bf16[256,2048]{1,0:T(8,128)(2,1)S(1)} %copy-done.7, bf16[2,256,2048]{2,1,0:T(8,128)(2,1)} %get-tuple-element.24.kv_ref, bf16[2,128,2048]{2,1,0:T(8,128)(2,1)} %collective-permute-done.17.rim_ref, s32[4,256,1]{2,1,0:T(8,128)S(1)} %copy.20.reach_ref, ...), custom_call_target="tpu_custom_call" | custom-call | flops 536870912 | bytes 5242880 | tf_op jit(solution)/shard_map/attend/pallas_call | solution.py:174
  159.7 15.0 %project.7 = (bf16[256,2048]{1,0:T(8,128)(2,1)S(1)}, bf16[2,256,2048]{2,1,0:T(8,128)(2,1)}, bf16[2,128,2048]{2,1,0:T(8,128)(2,1)}) custom-call(s32[5]{0:T(128)S(1)} %copy-done.10, bf16[4,256,2048]{2,1,0:T(8,128)(2,1)} %refs_1_.1, bf16[256,2048]{1,0:T(8,128)(2,1)} %collective-permute-done.15.rest_0_.refs_1_, ...), custom_call_target="tpu_custom_call" | custom-call | flops 4831838208 | bytes 26214400 | tf_op jit(solution)/shard_map/project/pallas_call | solution.py:103
  174.7 1.9 collective-permute-start.18
  176.6 0.5 collective-permute-start.19
  177.2 1.0 copy-done.8
  178.2 1.4 collective-permute-start.20
  179.5 19.3 %collective-permute-done.5.rest_0_.refs_1_ = bf16[256,2048]{1,0:T(8,128)(2,1)S(1)} collective-permute-done((bf16[256,2048]{1,0:T(8,128)(2,1)S(1)}, bf16[256,2048]{1,0:T(8,128)(2,1)S(1)}, u32[]{:S(2)}, u32[]{:S(2)}) %collective-permute-start.5) | collective-permute-done | bytes 1048608 | tf_op jit(solution)/shard_map/ppermute | solution.py:19
  198.8 1.2 copy-done.9
  200.0 5.7 %attend.4.refs_6_.rest_0_.refs_0_ = bf16[256,2048]{1,0:T(8,128)(2,1)S(1)} custom-call(bf16[256,2048]{1,0:T(8,128)(2,1)S(1)} %get-tuple-element.17.q_ref, bf16[2,256,2048]{2,1,0:T(8,128)(2,1)} %get-tuple-element.18.kv_ref, bf16[2,128,2048]{2,1,0:T(8,128)(2,1)S(1)} %copy-done.9, s32[4,256,1]{2,1,0:T(8,128)S(1)} %copy.20.reach_ref, ...), custom_call_target="tpu_custom_call" | custom-call | flops 536870912 | bytes 5242880 | tf_op jit(solution)/shard_map/attend/pallas_call | solution.py:174
  205.7 0.2 collective-permute-start.10
  205.9 14.3 %project.5 = (bf16[256,2048]{1,0:T(8,128)(2,1)S(1)}, bf16[2,256,2048]{2,1,0:T(8,128)(2,1)}, bf16[2,128,2048]{2,1,0:T(8,128)(2,1)}) custom-call(s32[5]{0:T(128)S(1)} %copy-done.10, bf16[4,256,2048]{2,1,0:T(8,128)(2,1)} %refs_1_.1, bf16[256,2048]{1,0:T(8,128)(2,1)S(1)} %collective-permute-done.5.rest_0_.refs_1_, ...), custom_call_target="tpu_custom_call" | custom-call | flops 4831838208 | bytes 26214400 | tf_op jit(solution)/shard_map/project/pallas_call | solution.py:103
  220.2 2.1 collective-permute-start.8
  222.3 1.9 collective-permute-start.9
  224.2 17.0 %collective-permute-done.19.rest_1_.refs_1_ = bf16[256,2048]{1,0:T(8,128)(2,1)S(1)} collective-permute-done((bf16[256,2048]{1,0:T(8,128)(2,1)S(1)}, bf16[256,2048]{1,0:T(8,128)(2,1)S(1)}, u32[]{:S(2)}, u32[]{:S(2)}) %collective-permute-start.19) | collective-permute-done | bytes 1048608 | tf_op jit(solution)/shard_map/ppermute | solution.py:19
  241.2 20.1 %collective-permute-done.20.rest_2_.refs_2_ = bf16[256,2048]{1,0:T(8,128)(2,1)S(1)} collective-permute-done((bf16[256,2048]{1,0:T(8,128)(2,1)S(1)}, bf16[256,2048]{1,0:T(8,128)(2,1)S(1)}, u32[]{:S(2)}, u32[]{:S(2)}) %collective-permute-start.20) | collective-permute-done | bytes 1048608 | tf_op jit(solution)/shard_map/ppermute | solution.py:19
  261.2 1.0 copy-done.2
  262.2 5.7 %attend.7.refs_5_.refs_0_ = bf16[256,2048]{1,0:T(8,128)(2,1)S(1)} custom-call(bf16[256,2048]{1,0:T(8,128)(2,1)S(1)} %get-tuple-element.26.q_ref, bf16[2,256,2048]{2,1,0:T(8,128)(2,1)} %get-tuple-element.27.kv_ref, bf16[2,128,2048]{2,1,0:T(8,128)(2,1)S(1)} %collective-permute-done.18.rim_ref, s32[4,256,1]{2,1,0:T(8,128)S(1)} %copy.20.reach_ref, ...), custom_call_target="tpu_custom_call" | custom-call | flops 536870912 | bytes 5242880 | tf_op jit(solution)/shard_map/attend/pallas_call | solution.py:174
  267.9 3.2 collective-permute-start.21
  271.2 3.7 collective-permute-start.22
  274.8 11.5 %collective-permute-done.10.rest_2_.refs_2_ = bf16[256,2048]{1,0:T(8,128)(2,1)S(1)} collective-permute-done((bf16[256,2048]{1,0:T(8,128)(2,1)S(1)}, bf16[256,2048]{1,0:T(8,128)(2,1)S(1)}, u32[]{:S(2)}, u32[]{:S(2)}) %collective-permute-start.10) | collective-permute-done | bytes 1048608 | tf_op jit(solution)/shard_map/ppermute | solution.py:19
  286.3 1.0 copy-done.4
  287.3 5.7 %attend.5.refs_6_.refs_0_.refs_4_ = bf16[256,2048]{1,0:T(8,128)(2,1)S(1)} custom-call(bf16[256,2048]{1,0:T(8,128)(2,1)S(1)} %get-tuple-element.20.q_ref, bf16[2,256,2048]{2,1,0:T(8,128)(2,1)} %get-tuple-element.21.kv_ref, bf16[2,128,2048]{2,1,0:T(8,128)(2,1)S(1)} %collective-permute-done.8.rim_ref, s32[4,256,1]{2,1,0:T(8,128)S(1)} %copy.20.reach_ref, ...), custom_call_target="tpu_custom_call" | custom-call | flops 536870912 | bytes 5242880 | tf_op jit(solution)/shard_map/attend/pallas_call | solution.py:174
  293.0 0.9 collective-permute-start.11
  293.9 3.4 collective-permute-start.12
  297.3 0.1 select_reduce_fusion
  297.5 8.9 %finish.3.refs_5_ = f32[4,256,2048]{2,1,0:T(8,128)} custom-call(s32[5]{0:T(128)S(1)} %copy-done.10, bf16[256,2048]{1,0:T(8,128)(2,1)S(1)} %attend.6.refs_6_.rest_0_.refs_0_, bf16[256,2048]{1,0:T(8,128)(2,1)S(1)} %collective-permute-done.19.rest_1_.refs_1_, bf16[256,2048]{1,0:T(8,128)(2,1)S(1)} %copy-done.3, bf16[4,256,2048]{2,1,0:T(8,128)(2,1)} %refs_1_.1, ...), custom_call_target="tpu_custom_call" | custom-call | flops 1610612736 | bytes 12582912 | tf_op jit(solution)/shard_map/finish/pallas_call | solution.py:223
  306.3 8.8 %finish.4.refs_5_ = f32[4,256,2048]{2,1,0:T(8,128)} custom-call(s32[5]{0:T(128)S(1)} %copy-done.10, bf16[256,2048]{1,0:T(8,128)(2,1)S(1)} %attend.4.refs_6_.rest_0_.refs_0_, bf16[256,2048]{1,0:T(8,128)(2,1)S(1)} %collective-permute-done.9.rest_1_.refs_1_, bf16[256,2048]{1,0:T(8,128)(2,1)S(1)} %copy-done.5, ...), custom_call_target="tpu_custom_call", output_to_operand_aliasing={{}: (6, {})} | custom-call | flops 1610612736 | bytes 12582912 | tf_op jit(solution)/shard_map/finish/pallas_call | solution.py:223
  315.2 18.6 %collective-permute-done.21.refs_1_ = bf16[256,2048]{1,0:T(8,128)(2,1)S(1)} collective-permute-done((bf16[256,2048]{1,0:T(8,128)(2,1)S(1)}, bf16[256,2048]{1,0:T(8,128)(2,1)S(1)}, u32[]{:S(2)}, u32[]{:S(2)}) %collective-permute-start.21) | collective-permute-done | bytes 1048608 | tf_op jit(solution)/shard_map/ppermute | solution.py:19
  333.8 8.8 %finish.5.refs_3_ = f32[4,256,2048]{2,1,0:T(8,128)} custom-call(s32[5]{0:T(128)S(1)} %copy-done.10, bf16[256,2048]{1,0:T(8,128)(2,1)S(1)} %attend.7.refs_5_.refs_0_, bf16[256,2048]{1,0:T(8,128)(2,1)S(1)} %collective-permute-done.21.refs_1_, bf16[256,2048]{1,0:T(8,128)(2,1)S(1)} %collective-permute-done.22.refs_2_, ...), custom_call_target="tpu_custom_call", output_to_operand_aliasing={{}: (6, {})} | custom-call | flops 1610612736 | bytes 12582912 | tf_op jit(solution)/shard_map/finish/pallas_call | solution.py:223
  342.6 8.2 %finish_near.1.refs_4_ = f32[4,256,2048]{2,1,0:T(8,128)} custom-call(s32[5]{0:T(128)S(1)} %broadcast_add_fusion.sec_ref, bf16[256,2048]{1,0:T(8,128)(2,1)S(1)} %attend.5.refs_6_.refs_0_.refs_4_, bf16[4,256,2048]{2,1,0:T(8,128)(2,1)S(1)} %copy-done.1, bf16[8,1536,256]{2,1,0:T(8,128)(2,1)} %bitcast.18, ...), custom_call_target="tpu_custom_call", output_to_operand_aliasing={{}: (4, {})} | custom-call | flops 1610612736 | bytes 10485760 | tf_op jit(solution)/shard_map/finish_near/pallas_call | solution.py:281
  350.8 25.2 %collective-permute-done.11.refs_0_ = bf16[256,2048]{1,0:T(8,128)(2,1)S(1)} collective-permute-done((bf16[256,2048]{1,0:T(8,128)(2,1)S(1)}, bf16[256,2048]{1,0:T(8,128)(2,1)S(1)}, u32[]{:S(2)}, u32[]{:S(2)}) %collective-permute-start.11) | collective-permute-done | bytes 1048608 | tf_op jit(solution)/shard_map/ppermute | solution.py:19
  376.0 0.1 collective-permute-done.12.refs_1_
  376.2 7.5 %finish_far.1 = f32[4,256,2048]{2,1,0:T(8,128)} custom-call(s32[5]{0:T(128)S(1)} %broadcast_add_fusion.sec_ref, bf16[256,2048]{1,0:T(8,128)(2,1)S(1)} %collective-permute-done.11.refs_0_, bf16[256,2048]{1,0:T(8,128)(2,1)S(1)} %collective-permute-done.12.refs_1_, bf16[8,1536,256]{2,1,0:T(8,128)(2,1)} %bitcast.19, ...), custom_call_target="tpu_custom_call", output_to_operand_aliasing={{}: (5, {})} | custom-call | flops 536870912 | bytes 8388608 | tf_op jit(solution)/shard_map/finish_far/pallas_call | solution.py:326
  (41 shorter events, 0.1 us)
Async XLA Ops:
  0.0 62.2 %copy-start.11 = (f32[2048]{0:T(1024)S(1)}, f32[2048]{0:T(1024)}, u32[]{:S(2)}) copy-start(f32[2048]{0:T(1024)} %param.7) | copy-start | bytes 24580
  3.8 2.2 copy-start
  6.0 58.5 %copy-start.10 = (s32[5]{0:T(128)S(1)}, s32[5]{0:T(128)}, u32[]{:S(2)}) copy-start(s32[5]{0:T(128)} %bits_ref.13) | copy-start | bytes 64
  7.1 55.2 %collective-permute-start.13 = (bf16[256,2048]{1,0:T(8,128)(2,1)}, bf16[256,2048]{1,0:T(8,128)(2,1)}, u32[]{:S(2)}, u32[]{:S(2)}) collective-permute-start(bf16[256,2048]{1,0:T(8,128)(2,1)} %stage.6), channel_id=1, source_target_pairs={{0,1},{1,0},{2,3},{3,2},{4,5},{5,4},{6,7},{7,6},{8,9},{9,8},{10,11... | collective-permute-start | bytes 3145736 | tf_op jit(solution)/shard_map/ppermute | solution.py:19
  8.6 53.6 %collective-permute-start.14 = (bf16[256,2048]{1,0:T(8,128)(2,1)}, bf16[256,2048]{1,0:T(8,128)(2,1)}, u32[]{:S(2)}, u32[]{:S(2)}) collective-permute-start(bf16[256,2048]{1,0:T(8,128)(2,1)} %stage.6), channel_id=1, source_target_pairs={{0,2},{1,3},{2,0},{3,1},{4,6},{5,7},{6,4},{7,5},{8,10},{9,11},{10,... | collective-permute-start | bytes 3145736 | tf_op jit(solution)/shard_map/ppermute | solution.py:19
  11.2 43.4 %collective-permute-start = (f32[3072]{0:T(1024)S(1)}, f32[3072]{0:T(1024)S(1)}, u32[]{:S(2)}, u32[]{:S(2)}) collective-permute-start(f32[3072]{0:T(1024)S(1)} %constant_dynamic-update-slice_fusion.rest_0_), channel_id=1, source_target_pairs={{0,1},{1,0},{2,3},{3,2},{4,5},{5,4},{6,7},{7,6},{8,9},{9,8},{10,11... | collective-permute-start | bytes 36872 | tf_op jit(solution)/shard_map/ppermute | solution.py:366
  11.7 46.1 %collective-permute-start.1 = (f32[3072]{0:T(1024)S(1)}, f32[3072]{0:T(1024)S(1)}, u32[]{:S(2)}, u32[]{:S(2)}) collective-permute-start(f32[3072]{0:T(1024)S(1)} %constant_dynamic-update-slice_fusion.rest_0_), channel_id=1, source_target_pairs={{0,2},{1,3},{2,0},{3,1},{4,6},{5,7},{6,4},{7,5},{8,10},{9,11},{10,... | collective-permute-start | bytes 36872 | tf_op jit(solution)/shard_map/ppermute | solution.py:366
  12.0 45.8 %collective-permute-start.2 = (f32[3072]{0:T(1024)S(1)}, f32[3072]{0:T(1024)S(1)}, u32[]{:S(2)}, u32[]{:S(2)}) collective-permute-start(f32[3072]{0:T(1024)S(1)} %constant_dynamic-update-slice_fusion.rest_0_), channel_id=1, source_target_pairs={{0,3},{1,2},{2,1},{3,0},{4,7},{5,6},{6,5},{7,4},{8,11},{9,10},{10,... | collective-permute-start | bytes 36872 | tf_op jit(solution)/shard_map/ppermute | solution.py:366
  58.9 67.3 %collective-permute-start.3 = (bf16[256,2048]{1,0:T(8,128)(2,1)}, bf16[256,2048]{1,0:T(8,128)(2,1)S(1)}, u32[]{:S(2)}, u32[]{:S(2)}) collective-permute-start(bf16[256,2048]{1,0:T(8,128)(2,1)} %stage.4), channel_id=1, source_target_pairs={{0,1},{1,0},{2,3},{3,2},{4,5},{5,4},{6,7},{7,6},{8,9},{9,8},{10,11... | collective-permute-start | bytes 3145736 | tf_op jit(solution)/shard_map/ppermute | solution.py:19
  59.6 66.7 %collective-permute-start.4 = (bf16[256,2048]{1,0:T(8,128)(2,1)}, bf16[256,2048]{1,0:T(8,128)(2,1)S(1)}, u32[]{:S(2)}, u32[]{:S(2)}) collective-permute-start(bf16[256,2048]{1,0:T(8,128)(2,1)} %stage.4), channel_id=1, source_target_pairs={{0,2},{1,3},{2,0},{3,1},{4,6},{5,7},{6,4},{7,5},{8,10},{9,11},{10,... | collective-permute-start | bytes 3145736 | tf_op jit(solution)/shard_map/ppermute | solution.py:19
  64.5 20.0 %copy-start.12 = (s32[4,256]{1,0:T(4,128)S(1)}, s32[4,256]{1,0:T(4,128)}, u32[]{:S(2)}) copy-start(s32[4,256]{1,0:T(4,128)} %param.11) | copy-start | bytes 12292
  79.5 1.0 copy-start.6
  80.6 63.3 %collective-permute-start.17 = (bf16[2,128,2048]{2,1,0:T(8,128)(2,1)}, bf16[2,128,2048]{2,1,0:T(8,128)(2,1)}, u32[]{:S(2)}, u32[]{:S(2)}) collective-permute-start(bf16[2,128,2048]{2,1,0:T(8,128)(2,1)} %get-tuple-element.25), channel_id=1, source_target_pairs={{0,4},{4,8},{8,12},{12,16},{16,20},{20,24},{24,28},{1,5},{5,9},{9,... | collective-permute-start | bytes 3145736 | tf_op jit(solution)/shard_map/ppermute | solution.py:25
  82.5 71.5 %collective-permute-start.15 = (bf16[256,2048]{1,0:T(8,128)(2,1)}, bf16[256,2048]{1,0:T(8,128)(2,1)}, u32[]{:S(2)}, u32[]{:S(2)}) collective-permute-start(bf16[256,2048]{1,0:T(8,128)(2,1)} %stage.7.refs_6_), channel_id=1, source_target_pairs={{0,1},{1,0},{2,3},{3,2},{4,5},{5,4},{6,7},{7,6},{8,9},{9,8},{10,11... | collective-permute-start | bytes 3145736 | tf_op jit(solution)/shard_map/ppermute | solution.py:19
  83.2 70.7 %collective-permute-start.16 = (bf16[256,2048]{1,0:T(8,128)(2,1)}, bf16[256,2048]{1,0:T(8,128)(2,1)}, u32[]{:S(2)}, u32[]{:S(2)}) collective-permute-start(bf16[256,2048]{1,0:T(8,128)(2,1)} %stage.7.refs_6_), channel_id=1, source_target_pairs={{0,2},{1,3},{2,0},{3,1},{4,6},{5,7},{6,4},{7,5},{8,10},{9,11},{10,... | collective-permute-start | bytes 3145736 | tf_op jit(solution)/shard_map/ppermute | solution.py:19
  127.5 26.5 %copy-start.7 = (bf16[256,2048]{1,0:T(8,128)(2,1)S(1)}, bf16[256,2048]{1,0:T(8,128)(2,1)}, u32[]{:S(2)}) copy-start(bf16[256,2048]{1,0:T(8,128)(2,1)} %copy-done.6) | copy-start | bytes 3145732
  141.8 35.3 %collective-permute-start.7 = (bf16[2,128,2048]{2,1,0:T(8,128)(2,1)}, bf16[2,128,2048]{2,1,0:T(8,128)(2,1)S(1)}, u32[]{:S(2)}, u32[]{:S(2)}) collective-permute-start(bf16[2,128,2048]{2,1,0:T(8,128)(2,1)} %get-tuple-element.19), channel_id=1, source_target_pairs={{0,4},{4,8},{8,12},{12,16},{16,20},{20,24},{24,28},{1,5},{5,9},{9,... | collective-permute-start | bytes 3145736 | tf_op jit(solution)/shard_map/ppermute | solution.py:25
  143.8 55.1 %collective-permute-start.5 = (bf16[256,2048]{1,0:T(8,128)(2,1)S(1)}, bf16[256,2048]{1,0:T(8,128)(2,1)S(1)}, u32[]{:S(2)}, u32[]{:S(2)}) collective-permute-start(bf16[256,2048]{1,0:T(8,128)(2,1)S(1)} %stage.5.refs_6_), channel_id=1, source_target_pairs={{0,1},{1,0},{2,3},{3,2},{4,5},{5,4},{6,7},{7,6},{8,9},{9,8},{10,11... | collective-permute-start | bytes 3145736 | tf_op jit(solution)/shard_map/ppermute | solution.py:19
  143.8 55.0 %collective-permute-start.6 = (bf16[256,2048]{1,0:T(8,128)(2,1)S(1)}, bf16[256,2048]{1,0:T(8,128)(2,1)S(1)}, u32[]{:S(2)}, u32[]{:S(2)}) collective-permute-start(bf16[256,2048]{1,0:T(8,128)(2,1)S(1)} %stage.5.refs_6_), channel_id=1, source_target_pairs={{0,2},{1,3},{2,0},{3,1},{4,6},{5,7},{6,4},{7,5},{8,10},{9,11},{10,... | collective-permute-start | bytes 3145736 | tf_op jit(solution)/shard_map/ppermute | solution.py:19
  174.7 47.6 %collective-permute-start.18 = (bf16[2,128,2048]{2,1,0:T(8,128)(2,1)}, bf16[2,128,2048]{2,1,0:T(8,128)(2,1)S(1)}, u32[]{:S(2)}, u32[]{:S(2)}) collective-permute-start(bf16[2,128,2048]{2,1,0:T(8,128)(2,1)} %get-tuple-element.28), channel_id=1, source_target_pairs={{0,4},{4,8},{8,12},{12,16},{16,20},{20,24},{24,28},{1,5},{5,9},{9,... | collective-permute-start | bytes 3145736 | tf_op jit(solution)/shard_map/ppermute | solution.py:25
  176.6 64.5 %collective-permute-start.19 = (bf16[256,2048]{1,0:T(8,128)(2,1)S(1)}, bf16[256,2048]{1,0:T(8,128)(2,1)S(1)}, u32[]{:S(2)}, u32[]{:S(2)}) collective-permute-start(bf16[256,2048]{1,0:T(8,128)(2,1)S(1)} %attend.6.refs_6_.rest_0_.refs_0_), channel_id=1, source_target_pairs={{0,1},{1,0},{2,3},{3,2},{4,5},{5,4},{6,7},{7,6},{8,9},{9,8},{10,11... | collective-permute-start | bytes 3145736 | tf_op jit(solution)/shard_map/ppermute | solution.py:19
  177.2 1.0 copy-start.8
  178.2 83.1 %collective-permute-start.20 = (bf16[256,2048]{1,0:T(8,128)(2,1)S(1)}, bf16[256,2048]{1,0:T(8,128)(2,1)S(1)}, u32[]{:S(2)}, u32[]{:S(2)}) collective-permute-start(bf16[256,2048]{1,0:T(8,128)(2,1)S(1)} %attend.6.refs_6_.rest_0_.refs_0_), channel_id=1, source_target_pairs={{0,2},{1,3},{2,0},{3,1},{4,6},{5,7},{6,4},{7,5},{8,10},{9,11},{10,... | collective-permute-start | bytes 3145736 | tf_op jit(solution)/shard_map/ppermute | solution.py:19
  198.8 1.2 copy-start.9
  205.7 80.6 %collective-permute-start.10 = (bf16[256,2048]{1,0:T(8,128)(2,1)S(1)}, bf16[256,2048]{1,0:T(8,128)(2,1)S(1)}, u32[]{:S(2)}, u32[]{:S(2)}) collective-permute-start(bf16[256,2048]{1,0:T(8,128)(2,1)S(1)} %attend.4.refs_6_.rest_0_.refs_0_), channel_id=1, source_target_pairs={{0,2},{1,3},{2,0},{3,1},{4,6},{5,7},{6,4},{7,5},{8,10},{9,11},{10,... | collective-permute-start | bytes 3145736 | tf_op jit(solution)/shard_map/ppermute | solution.py:19
  220.2 54.6 %collective-permute-start.8 = (bf16[2,128,2048]{2,1,0:T(8,128)(2,1)}, bf16[2,128,2048]{2,1,0:T(8,128)(2,1)S(1)}, u32[]{:S(2)}, u32[]{:S(2)}) collective-permute-start(bf16[2,128,2048]{2,1,0:T(8,128)(2,1)} %get-tuple-element.22), channel_id=1, source_target_pairs={{0,4},{4,8},{8,12},{12,16},{16,20},{20,24},{24,28},{1,5},{5,9},{9,... | collective-permute-start | bytes 3145736 | tf_op jit(solution)/shard_map/ppermute | solution.py:25
  222.3 64.0 %collective-permute-start.9 = (bf16[256,2048]{1,0:T(8,128)(2,1)S(1)}, bf16[256,2048]{1,0:T(8,128)(2,1)S(1)}, u32[]{:S(2)}, u32[]{:S(2)}) collective-permute-start(bf16[256,2048]{1,0:T(8,128)(2,1)S(1)} %attend.4.refs_6_.rest_0_.refs_0_), channel_id=1, source_target_pairs={{0,1},{1,0},{2,3},{3,2},{4,5},{5,4},{6,7},{7,6},{8,9},{9,8},{10,11... | collective-permute-start | bytes 3145736 | tf_op jit(solution)/shard_map/ppermute | solution.py:19
  261.2 1.0 copy-start.2
  267.9 29.6 %copy-start.3 = (bf16[256,2048]{1,0:T(8,128)(2,1)S(1)}, bf16[256,2048]{1,0:T(8,128)(2,1)}, u32[]{:S(2)}) copy-start(bf16[256,2048]{1,0:T(8,128)(2,1)} %copy-done.2) | copy-start | bytes 3145732
  267.9 65.8 %collective-permute-start.21 = (bf16[256,2048]{1,0:T(8,128)(2,1)S(1)}, bf16[256,2048]{1,0:T(8,128)(2,1)S(1)}, u32[]{:S(2)}, u32[]{:S(2)}) collective-permute-start(bf16[256,2048]{1,0:T(8,128)(2,1)S(1)} %attend.7.refs_5_.refs_0_), channel_id=1, source_target_pairs={{0,1},{1,0},{2,3},{3,2},{4,5},{5,4},{6,7},{7,6},{8,9},{9,8},{10,11... | collective-permute-start | bytes 3145736 | tf_op jit(solution)/shard_map/ppermute | solution.py:19
  271.2 62.6 %collective-permute-start.22 = (bf16[256,2048]{1,0:T(8,128)(2,1)S(1)}, bf16[256,2048]{1,0:T(8,128)(2,1)S(1)}, u32[]{:S(2)}, u32[]{:S(2)}) collective-permute-start(bf16[256,2048]{1,0:T(8,128)(2,1)S(1)} %attend.7.refs_5_.refs_0_), channel_id=1, source_target_pairs={{0,2},{1,3},{2,0},{3,1},{4,6},{5,7},{6,4},{7,5},{8,10},{9,11},{10,... | collective-permute-start | bytes 3145736 | tf_op jit(solution)/shard_map/ppermute | solution.py:19
  286.3 1.0 copy-start.4
  293.0 83.1 %collective-permute-start.11 = (bf16[256,2048]{1,0:T(8,128)(2,1)S(1)}, bf16[256,2048]{1,0:T(8,128)(2,1)S(1)}, u32[]{:S(2)}, u32[]{:S(2)}) collective-permute-start(bf16[256,2048]{1,0:T(8,128)(2,1)S(1)} %attend.5.refs_6_.refs_0_.refs_4_), channel_id=1, source_target_pairs={{0,1},{1,0},{2,3},{3,2},{4,5},{5,4},{6,7},{7,6},{8,9},{9,8},{10,11... | collective-permute-start | bytes 3145736 | tf_op jit(solution)/shard_map/ppermute | solution.py:19
  293.9 82.3 %collective-permute-start.12 = (bf16[256,2048]{1,0:T(8,128)(2,1)S(1)}, bf16[256,2048]{1,0:T(8,128)(2,1)S(1)}, u32[]{:S(2)}, u32[]{:S(2)}) collective-permute-start(bf16[256,2048]{1,0:T(8,128)(2,1)S(1)} %attend.5.refs_6_.refs_0_.refs_4_), channel_id=1, source_target_pairs={{0,2},{1,3},{2,0},{3,1},{4,6},{5,7},{6,4},{7,5},{8,10},{9,11},{10,... | collective-permute-start | bytes 3145736 | tf_op jit(solution)/shard_map/ppermute | solution.py:19
  297.5 8.9 %copy-start.5 = (bf16[256,2048]{1,0:T(8,128)(2,1)S(1)}, bf16[256,2048]{1,0:T(8,128)(2,1)}, u32[]{:S(2)}) copy-start(bf16[256,2048]{1,0:T(8,128)(2,1)} %copy-done.4) | copy-start | bytes 3145732
  315.2 27.4 %copy-start.1 = (bf16[4,256,2048]{2,1,0:T(8,128)(2,1)S(1)}, bf16[4,256,2048]{2,1,0:T(8,128)(2,1)}, u32[]{:S(2)}) copy-start(bf16[4,256,2048]{2,1,0:T(8,128)(2,1)} %refs_1_.1) | copy-start | bytes 12582916
